TPU v7x, 32 devices: a whole 2x2x4 slice. The times are simulated.
32 devices in a mesh: pencil: 2 (over core), gz: 4 (over y, x), coarse: 4 (over z).
Axes of the slice: x: 2, y: 2, z: 4, core: 2. Of those that a mesh axis runs over, the one named last changes fastest.
Arguments:
- right_side: float32 [16, 64, 1024], P('pencil', 'coarse', 'gz'), may hold values from -6 to 6
- conductivity: float32 [16, 64, 1024], P('pencil', 'coarse', 'gz'), may hold values from 0.2 to 5
- guess: float32 [16, 64, 1024], P('pencil', 'coarse', 'gz'), may hold values from -4 to 4
Outputs:
- updated: float32 [16, 64, 1024], P('pencil', 'coarse', 'gz')
- smoothed_residual: float32 [16, 64, 1024], P('pencil', 'coarse', 'gz')
All inputs are finite; a program needn't handle non-finite values.
Results may differ from a plain program's by a relative error of at most 0.00002.
Values sent between devices are 32-bit elements; how exact they have to be, the bound alone decides.
A program may use at most 64 MiB of HBM per device.

v0:
```python
import jax
import jax.numpy as jnp
from jax import lax
from jax.sharding import PartitionSpec as P

KSWEEP = 4


def padded_2(cells, sides, width):
    for axis, dim in sides:
        count = lax.axis_size(axis)
        ends = count - 1
        head = lax.slice_in_dim(cells, 0, width, axis=dim)
        tail = lax.slice_in_dim(cells, cells.shape[dim] - width, cells.shape[dim], axis=dim)
        cells = jnp.concatenate(
            [
                lax.ppermute(tail, axis, [(i, (i + 1) % count) for i in range(ends)]),
                cells,
                lax.ppermute(head, axis, [((i + 1) % count, i) for i in range(ends)]),
            ],
            axis=dim,
        )
    return cells


def face_terms(padded_k, scale):
    k = padded_k[1:-1, 1:-1, 1:-1]
    return [
        scale * 0.5 * (k + padded_k[:-2, 1:-1, 1:-1]),
        scale * 0.5 * (k + padded_k[2:, 1:-1, 1:-1]),
        scale * 0.5 * (k + padded_k[1:-1, :-2, 1:-1]),
        scale * 0.5 * (k + padded_k[1:-1, 2:, 1:-1]),
        scale * 0.5 * (k + padded_k[1:-1, 1:-1, :-2]),
        scale * 0.5 * (k + padded_k[1:-1, 1:-1, 2:]),
    ]


def diagonal_of(terms):
    return terms[0] + terms[1] + terms[2] + terms[3] + terms[4] + terms[5]


def operate(padded_v, terms, diag):
    v = padded_v[1:-1, 1:-1, 1:-1]
    out = diag * v - terms[0] * padded_v[:-2, 1:-1, 1:-1] - terms[1] * padded_v[2:, 1:-1, 1:-1]
    out = out - terms[2] * padded_v[1:-1, :-2, 1:-1] - terms[3] * padded_v[1:-1, 2:, 1:-1]
    return out - terms[4] * padded_v[1:-1, 1:-1, :-2] - terms[5] * padded_v[1:-1, 1:-1, 2:]


def restrict(field):
    a, b, c = field.shape
    return field.reshape(a // 2, 2, b // 2, 2, c // 2, 2).mean(axis=(1, 3, 5))


def extend_faces(stacked):
    return padded_2(stacked, (("pencil", 1), ("gz", 3), ("coarse", 2)), 1)


def extend_lined(stacked):
    padded = padded_2(stacked, (("gz", 3), ("coarse", 2)), 1)
    return jnp.pad(padded, ((0, 0), (1, 1), (0, 0), (0, 0)))


def coarse_solve(coarse_r, coarse_k, extend):
    cterms = face_terms(extend(coarse_k[None])[0], 0.25)
    dcoarse = diagonal_of(cterms)
    correction = 0.8 * coarse_r / dcoarse
    for sweep in range(KSWEEP - 1):
        padded = extend(correction[None])[0]
        correction = correction + 0.8 * (coarse_r - operate(padded, cterms, dcoarse)) / dcoarse
    return correction


def on_device(right_side, conductivity, guess):
    theta = 1.1
    delta = 0.8
    sigma = theta / delta
    rho0 = 1.0 / sigma
    rho1 = 1.0 / (2.0 * sigma - rho0)
    first = extend_faces(jnp.stack([guess, conductivity]))
    terms = face_terms(first[1], 1.0)
    dfine = diagonal_of(terms)
    r0 = right_side - operate(first[0], terms, dfine)
    d0 = r0 / (theta * dfine)
    r1 = r0 - operate(extend_faces(d0[None])[0], terms, dfine)
    d1 = rho1 * rho0 * d0 + 2.0 * rho1 / delta * r1 / dfine
    smoothed = r1 - operate(extend_faces(d1[None])[0], terms, dfine)
    coarse_r = restrict(r0)
    coarse_k = restrict(conductivity)
    half_x, half_y, half_z = coarse_r.shape
    whole_r, whole_k = (
        lax.all_gather(coarse_r, "pencil", axis=0, tiled=True),
        lax.all_gather(coarse_k, "pencil", axis=0, tiled=True),
    )
    line_correction = coarse_solve(whole_r, whole_k, extend_lined)
    correction = lax.dynamic_slice_in_dim(
        line_correction, lax.axis_index("pencil") * half_x, half_x, 0
    )
    lifted = jnp.repeat(jnp.repeat(jnp.repeat(correction, 2, axis=0), 2, axis=1), 2, axis=2)
    updated = guess + d0 + d1 + lifted
    return (updated, smoothed)


def solution(mesh):
    return jax.shard_map(
        on_device,
        mesh=mesh,
        in_specs=(
            P("pencil", "coarse", "gz"),
            P("pencil", "coarse", "gz"),
            P("pencil", "coarse", "gz"),
        ),
        out_specs=(P("pencil", "coarse", "gz"), P("pencil", "coarse", "gz")),
        check_vma=False,
    )
```

profile of v0, /device:TPU:0, one launch (start us, length us, event | category | flops | bytes accessed | tf_op | source)
XLA Modules:
  0.0 157.1 jit_solution(2288869807780425876)
XLA Ops:
  0.6 0.8 pad_maximum_fusion.5
  1.4 2.3 %collective-permute-start = (f32[2,1,16,256]{3,2,1,0:T(8,128)S(1)}, f32[2,1,16,256]{3,2,1,0:T(8,128)S(1)}, u32[]{:S(2)}, u32[]{:S(2)}) collective-permute-start(f32[2,1,16,256]{3,2,1,0:T(8,128)S(1)} %get-tuple-element.41), channel_id=1, source_target_pairs={{0,16},{1,17},{2,18},{3,19},{4,20},{5,21},{6,22},{7,23},{8,24},{9,... | collective-permute-start | bytes 98312 | tf_op jit(solution)/shard_map/ppermute | solution.py:17
  3.8 1.4 collective-permute-start.1
  5.2 10.5 %reshape.20 = f32[4,2,8,2,128,2]{5,4,3,2,1,0:T(8,128)} reshape(f32[8,16,256]{2,1,0:T(8,128)} %param.4) | data formatting | bytes 262144 | tf_op jit(solution)/shard_map/reshape | solution.py:51
  15.8 4.1 %reduce_sum.19 = f32[4,8,128]{2,1,0:T(8,128)S(1)} reduce(f32[4,2,8,2,128,2]{5,4,3,2,1,0:T(8,128)} %reshape.20, f32[]{:T(128)} %constant.8.clone.1), dimensions={1,3,5}, to_apply=%region_1.0 | reduce | flops 28672 | bytes 147460 | tf_op jit(solution)/shard_map/reduce_sum | solution.py:51
  19.8 2.6 %all_gather.7 = f32[8,8,128]{2,1,0:T(8,128)S(1)} all-gather(f32[4,8,128]{2,1,0:T(8,128)S(1)} %broadcast_multiply_fusion), channel_id=1, replica_groups=mesh['pencil'=2,'gz'=4,'coarse'=4] {'pencil'}, dimensions={0}, use_global_device_ids=true | all-gather | bytes 49152 | tf_op jit(solution)/shard_map/all_gather | solution.py:92
  22.5 4.2 %collective-permute-start.12 = (f32[1,8,8,1]{3,2,1,0:T(8,128)S(1)}, f32[1,8,8,1]{3,2,1,0:T(8,128)S(1)}, u32[]{:S(2)}, u32[]{:S(2)}) collective-permute-start(f32[1,8,8,1]{3,2,1,0:T(8,128)S(1)} %get-tuple-element.68), channel_id=1, source_target_pairs={{0,4},{4,8},{8,12},{1,5},{5,9},{9,13},{2,6},{6,10},{10,14},{3,7},{... | collective-permute-start | bytes 776 | tf_op jit(solution)/shard_map/ppermute | solution.py:17
  26.7 1.3 collective-permute-start.13
  28.2 4.6 %collective-permute-start.2 = (f32[2,10,16,1]{3,2,1,0:T(8,128)S(1)}, f32[2,10,16,1]{3,2,1,0:T(8,128)S(1)}, u32[]{:S(2)}, u32[]{:S(2)}) collective-permute-start(f32[2,10,16,1]{3,2,1,0:T(8,128)S(1)} %get-tuple-element.37), channel_id=1, source_target_pairs={{0,4},{4,8},{8,12},{1,5},{5,9},{9,13},{2,6},{6,10},{10,14},{3,7},{... | collective-permute-start | bytes 3848 | tf_op jit(solution)/shard_map/ppermute | solution.py:17
  32.8 1.3 collective-permute-start.3
  34.2 3.5 %collective-permute-start.14 = (f32[1,8,1,130]{3,2,1,0:T(1,128)S(1)}, f32[1,8,1,130]{3,2,1,0:T(1,128)S(1)}, u32[]{:S(2)}, u32[]{:S(2)}) collective-permute-start(f32[1,8,1,130]{3,2,1,0:T(1,128)S(1)} %get-tuple-element.60), channel_id=1, source_target_pairs={{0,1},{1,2},{2,3},{4,5},{5,6},{6,7},{8,9},{9,10},{10,11},{12,13},{... | collective-permute-start | bytes 12488 | tf_op jit(solution)/shard_map/ppermute | solution.py:17
  37.7 1.3 collective-permute-start.15
  39.0 3.5 %collective-permute-done.3 = f32[2,10,16,1]{3,2,1,0:T(8,128)S(1)} collective-permute-done((f32[2,10,16,1]{3,2,1,0:T(8,128)S(1)}, f32[2,10,16,1]{3,2,1,0:T(8,128)S(1)}, u32[]{:S(2)}, u32[]{:S(2)}) %collective-permute-start.3) | collective-permute-done | bytes 1312 | tf_op jit(solution)/shard_map/ppermute | solution.py:19
  42.5 0.2 pad_maximum_fusion.11
  42.8 3.5 %collective-permute-start.4 = (f32[2,10,1,258]{3,0,2,1:T(2,128)S(1)}, f32[2,10,1,258]{3,0,2,1:T(2,128)S(1)}, u32[]{:S(2)}, u32[]{:S(2)}) collective-permute-start(f32[2,10,1,258]{3,0,2,1:T(2,128)S(1)} %copy.77), channel_id=1, source_target_pairs={{0,1},{1,2},{2,3},{4,5},{5,6},{6,7},{8,9},{9,10},{10,11},{12,13},{... | collective-permute-start | bytes 61928 | tf_op jit(solution)/shard_map/ppermute | solution.py:17
  46.3 1.3 collective-permute-start.5
  47.9 4.2 %collective-permute-done.5 = f32[2,10,1,258]{3,0,2,1:T(2,128)S(1)} collective-permute-done((f32[2,10,1,258]{3,0,2,1:T(2,128)S(1)}, f32[2,10,1,258]{3,0,2,1:T(2,128)S(1)}, u32[]{:S(2)}, u32[]{:S(2)}) %collective-permute-start.5) | collective-permute-done | bytes 20672 | tf_op jit(solution)/shard_map/ppermute | solution.py:19
  52.1 0.3 pad_maximum_fusion
  52.5 0.5 fusion.66
  53.0 9.8 %reshape.19 = f32[4,2,8,2,128,2]{5,4,3,2,1,0:T(8,128)} reshape(f32[8,16,256]{2,1,0:T(8,128)S(1)} %get-tuple-element.13) | data formatting | bytes 262144 | tf_op jit(solution)/shard_map/reshape | solution.py:51
  62.8 4.0 %reduce_sum.18 = f32[4,8,128]{2,1,0:T(8,128)S(1)} reduce(f32[4,2,8,2,128,2]{5,4,3,2,1,0:T(8,128)} %reshape.19, f32[]{:T(128)} %constant.8.clone.1), dimensions={1,3,5}, to_apply=%region_0.0 | reduce | flops 28672 | bytes 147460 | tf_op jit(solution)/shard_map/reduce_sum | solution.py:51
  66.8 1.8 %all_gather.6 = f32[8,8,128]{2,1,0:T(8,128)S(1)} all-gather(f32[4,8,128]{2,1,0:T(8,128)S(1)} %broadcast_multiply_fusion.1), channel_id=1, replica_groups=mesh['pencil'=2,'gz'=4,'coarse'=4] {'pencil'}, dimensions={0}, use_global_device_ids=true | all-gather | bytes 49152 | tf_op jit(solution)/shard_map/all_gather | solution.py:91
  68.9 2.9 %collective-permute-start.16 = (f32[1,8,8,1]{3,2,1,0:T(8,128)S(1)}, f32[1,8,8,1]{3,2,1,0:T(8,128)S(1)}, u32[]{:S(2)}, u32[]{:S(2)}) collective-permute-start(f32[1,8,8,1]{3,2,1,0:T(8,128)S(1)} %get-tuple-element.66), channel_id=1, source_target_pairs={{0,4},{4,8},{8,12},{1,5},{5,9},{9,13},{2,6},{6,10},{10,14},{3,7},{... | collective-permute-start | bytes 776 | tf_op jit(solution)/shard_map/ppermute | solution.py:17
  71.8 1.3 collective-permute-start.17
  73.1 0.3 collective-permute-done.16
  73.4 4.7 %collective-permute-done.17 = f32[1,8,8,1]{3,2,1,0:T(8,128)S(1)} collective-permute-done((f32[1,8,8,1]{3,2,1,0:T(8,128)S(1)}, f32[1,8,8,1]{3,2,1,0:T(8,128)S(1)}, u32[]{:S(2)}, u32[]{:S(2)}) %collective-permute-start.17) | collective-permute-done | bytes 288 | tf_op jit(solution)/shard_map/ppermute | solution.py:19
  78.2 3.5 %collective-permute-start.18 = (f32[1,8,1,130]{3,2,1,0:T(1,128)S(1)}, f32[1,8,1,130]{3,2,1,0:T(1,128)S(1)}, u32[]{:S(2)}, u32[]{:S(2)}) collective-permute-start(f32[1,8,1,130]{3,2,1,0:T(1,128)S(1)} %get-tuple-element.58), channel_id=1, source_target_pairs={{0,1},{1,2},{2,3},{4,5},{5,6},{6,7},{8,9},{9,10},{10,11},{12,13},{... | collective-permute-start | bytes 12488 | tf_op jit(solution)/shard_map/ppermute | solution.py:17
  81.7 1.3 collective-permute-start.19
  83.0 4.2 %collective-permute-done.19 = f32[1,8,1,130]{3,2,1,0:T(1,128)S(1)} collective-permute-done((f32[1,8,1,130]{3,2,1,0:T(1,128)S(1)}, f32[1,8,1,130]{3,2,1,0:T(1,128)S(1)}, u32[]{:S(2)}, u32[]{:S(2)}) %collective-permute-start.19) | collective-permute-done | bytes 4192 | tf_op jit(solution)/shard_map/ppermute | solution.py:19
  87.6 4.8 %collective-permute-start.20 = (f32[1,8,8,1]{3,2,1,0:T(8,128)S(1)}, f32[1,8,8,1]{3,2,1,0:T(8,128)S(1)}, u32[]{:S(2)}, u32[]{:S(2)}) collective-permute-start(f32[1,8,8,1]{3,2,1,0:T(8,128)S(1)} %get-tuple-element.64), channel_id=1, source_target_pairs={{0,4},{4,8},{8,12},{1,5},{5,9},{9,13},{2,6},{6,10},{10,14},{3,7},{... | collective-permute-start | bytes 776 | tf_op jit(solution)/shard_map/ppermute | solution.py:17
  92.4 1.3 collective-permute-start.21
  93.7 0.3 collective-permute-done.20
  94.0 4.2 %collective-permute-done.21 = f32[1,8,8,1]{3,2,1,0:T(8,128)S(1)} collective-permute-done((f32[1,8,8,1]{3,2,1,0:T(8,128)S(1)}, f32[1,8,8,1]{3,2,1,0:T(8,128)S(1)}, u32[]{:S(2)}, u32[]{:S(2)}) %collective-permute-start.21) | collective-permute-done | bytes 288 | tf_op jit(solution)/shard_map/ppermute | solution.py:19
  98.3 3.5 %collective-permute-start.22 = (f32[1,8,1,130]{3,2,1,0:T(1,128)S(1)}, f32[1,8,1,130]{3,2,1,0:T(1,128)S(1)}, u32[]{:S(2)}, u32[]{:S(2)}) collective-permute-start(f32[1,8,1,130]{3,2,1,0:T(1,128)S(1)} %get-tuple-element.56), channel_id=1, source_target_pairs={{0,1},{1,2},{2,3},{4,5},{5,6},{6,7},{8,9},{9,10},{10,11},{12,13},{... | collective-permute-start | bytes 12488 | tf_op jit(solution)/shard_map/ppermute | solution.py:17
  101.8 1.3 collective-permute-start.23
  103.1 1.3 collective-permute-start.6
  104.4 1.3 collective-permute-start.7
  105.7 1.6 %collective-permute-done.23 = f32[1,8,1,130]{3,2,1,0:T(1,128)S(1)} collective-permute-done((f32[1,8,1,130]{3,2,1,0:T(1,128)S(1)}, f32[1,8,1,130]{3,2,1,0:T(1,128)S(1)}, u32[]{:S(2)}, u32[]{:S(2)}) %collective-permute-start.23) | collective-permute-done | bytes 4192 | tf_op jit(solution)/shard_map/ppermute | solution.py:19
  107.7 2.8 %collective-permute-start.8 = (f32[1,10,16,1]{3,2,1,0:T(8,128)S(1)}, f32[1,10,16,1]{3,2,1,0:T(8,128)S(1)}, u32[]{:S(2)}, u32[]{:S(2)}) collective-permute-start(f32[1,10,16,1]{3,2,1,0:T(8,128)S(1)} %get-tuple-element.45), channel_id=1, source_target_pairs={{0,4},{4,8},{8,12},{1,5},{5,9},{9,13},{2,6},{6,10},{10,14},{3,7},{... | collective-permute-start | bytes 1928 | tf_op jit(solution)/shard_map/ppermute | solution.py:17
  110.6 1.3 collective-permute-start.9
  111.9 4.5 %collective-permute-start.24 = (f32[1,8,8,1]{3,2,1,0:T(8,128)S(1)}, f32[1,8,8,1]{3,2,1,0:T(8,128)S(1)}, u32[]{:S(2)}, u32[]{:S(2)}) collective-permute-start(f32[1,8,8,1]{3,2,1,0:T(8,128)S(1)} %get-tuple-element.62), channel_id=1, source_target_pairs={{0,4},{4,8},{8,12},{1,5},{5,9},{9,13},{2,6},{6,10},{10,14},{3,7},{... | collective-permute-start | bytes 776 | tf_op jit(solution)/shard_map/ppermute | solution.py:17
  116.5 1.3 collective-permute-start.25
  117.8 0.2 pad_maximum_fusion.21
  118.0 4.4 %collective-permute-start.10 = (f32[1,10,1,258]{3,2,1,0:T(1,128)S(1)}, f32[1,10,1,258]{3,2,1,0:T(1,128)S(1)}, u32[]{:S(2)}, u32[]{:S(2)}) collective-permute-start(f32[1,10,1,258]{3,2,1,0:T(1,128)S(1)} %get-tuple-element.35), channel_id=1, source_target_pairs={{0,1},{1,2},{2,3},{4,5},{5,6},{6,7},{8,9},{9,10},{10,11},{12,13},{... | collective-permute-start | bytes 30968 | tf_op jit(solution)/shard_map/ppermute | solution.py:17
  122.4 1.3 collective-permute-start.11
  123.8 4.5 %collective-permute-start.26 = (f32[1,8,1,130]{3,2,1,0:T(1,128)S(1)}, f32[1,8,1,130]{3,2,1,0:T(1,128)S(1)}, u32[]{:S(2)}, u32[]{:S(2)}) collective-permute-start(f32[1,8,1,130]{3,2,1,0:T(1,128)S(1)} %get-tuple-element.54), channel_id=1, source_target_pairs={{0,1},{1,2},{2,3},{4,5},{5,6},{6,7},{8,9},{9,10},{10,11},{12,13},{... | collective-permute-start | bytes 12488 | tf_op jit(solution)/shard_map/ppermute | solution.py:17
  128.4 1.3 collective-permute-start.27
  129.7 0.2 maximum_bitcast_fusion
  129.9 0.3 fusion.65
  130.2 1.3 collective-permute-start.28
  131.5 1.3 collective-permute-start.29
  132.8 1.1 collective-permute-done.27
  134.1 0.5 collective-permute-done.29
  134.7 4.6 %collective-permute-start.30 = (f32[1,10,16,1]{3,2,1,0:T(8,128)S(1)}, f32[1,10,16,1]{3,2,1,0:T(8,128)S(1)}, u32[]{:S(2)}, u32[]{:S(2)}) collective-permute-start(f32[1,10,16,1]{3,2,1,0:T(8,128)S(1)} %get-tuple-element.43), channel_id=1, source_target_pairs={{0,4},{4,8},{8,12},{1,5},{5,9},{9,13},{2,6},{6,10},{10,14},{3,7},{... | collective-permute-start | bytes 1928 | tf_op jit(solution)/shard_map/ppermute | solution.py:17
  139.3 1.3 collective-permute-start.31
  140.7 0.6 collective-permute-done.30
  141.3 4.3 %collective-permute-done.31 = f32[1,10,16,1]{3,2,1,0:T(8,128)S(1)} collective-permute-done((f32[1,10,16,1]{3,2,1,0:T(8,128)S(1)}, f32[1,10,16,1]{3,2,1,0:T(8,128)S(1)}, u32[]{:S(2)}, u32[]{:S(2)}) %collective-permute-start.31) | collective-permute-done | bytes 672 | tf_op jit(solution)/shard_map/ppermute | solution.py:19
  145.8 4.5 %collective-permute-start.32 = (f32[1,10,1,258]{3,2,1,0:T(1,128)S(1)}, f32[1,10,1,258]{3,2,1,0:T(1,128)S(1)}, u32[]{:S(2)}, u32[]{:S(2)}) collective-permute-start(f32[1,10,1,258]{3,2,1,0:T(1,128)S(1)} %get-tuple-element.33), channel_id=1, source_target_pairs={{0,1},{1,2},{2,3},{4,5},{5,6},{6,7},{8,9},{9,10},{10,11},{12,13},{... | collective-permute-start | bytes 30968 | tf_op jit(solution)/shard_map/ppermute | solution.py:17
  150.3 1.3 collective-permute-start.33
  151.7 0.2 copy.75
  152.0 0.4 copy.76
  152.4 3.6 %collective-permute-done.33 = f32[1,10,1,258]{3,2,1,0:T(1,128)S(1)} collective-permute-done((f32[1,10,1,258]{3,2,1,0:T(1,128)S(1)}, f32[1,10,1,258]{3,2,1,0:T(1,128)S(1)}, u32[]{:S(2)}, u32[]{:S(2)}) %collective-permute-start.33) | collective-permute-done | bytes 10352 | tf_op jit(solution)/shard_map/ppermute | solution.py:19
  155.9 0.2 maximum_bitcast_fusion.1
  156.1 1.0 fusion.6
  (64 shorter events, 2.7 us)
Async XLA Ops:
  1.4 26.6 %collective-permute-start = (f32[2,1,16,256]{3,2,1,0:T(8,128)S(1)}, f32[2,1,16,256]{3,2,1,0:T(8,128)S(1)}, u32[]{:S(2)}, u32[]{:S(2)}) collective-permute-start(f32[2,1,16,256]{3,2,1,0:T(8,128)S(1)} %get-tuple-element.41), channel_id=1, source_target_pairs={{0,16},{1,17},{2,18},{3,19},{4,20},{5,21},{6,22},{7,23},{8,24},{9,... | collective-permute-start | bytes 98312 | tf_op jit(solution)/shard_map/ppermute | solution.py:17
  3.8 24.3 %copy-start = (f32[8,16,256]{2,1,0:T(8,128)S(1)}, f32[8,16,256]{2,1,0:T(8,128)}, u32[]{:S(2)}) copy-start(f32[8,16,256]{2,1,0:T(8,128)} %param.4) | copy-start | bytes 393220
  3.8 24.3 %copy-start.1 = (f32[8,16,256]{2,1,0:T(8,128)S(1)}, f32[8,16,256]{2,1,0:T(8,128)}, u32[]{:S(2)}) copy-start(f32[8,16,256]{2,1,0:T(8,128)} %param.5) | copy-start | bytes 393220
  3.8 24.3 %collective-permute-start.1 = (f32[2,1,16,256]{3,2,1,0:T(8,128)S(1)}, f32[2,1,16,256]{3,2,1,0:T(8,128)S(1)}, u32[]{:S(2)}, u32[]{:S(2)}) collective-permute-start(f32[2,1,16,256]{3,2,1,0:T(8,128)S(1)} %get-tuple-element.42), channel_id=1, source_target_pairs={{16,0},{17,1},{18,2},{19,3},{20,4},{21,5},{22,6},{23,7},{24,8},{25... | collective-permute-start | bytes 98312 | tf_op jit(solution)/shard_map/ppermute | solution.py:19
  15.7 36.8 %copy-start.2 = (f32[8,16,256]{2,1,0:T(8,128)S(1)}, f32[8,16,256]{2,1,0:T(8,128)}, u32[]{:S(2)}) copy-start(f32[8,16,256]{2,1,0:T(8,128)} %param.3) | copy-start | bytes 393220
  22.5 11.6 %collective-permute-start.12 = (f32[1,8,8,1]{3,2,1,0:T(8,128)S(1)}, f32[1,8,8,1]{3,2,1,0:T(8,128)S(1)}, u32[]{:S(2)}, u32[]{:S(2)}) collective-permute-start(f32[1,8,8,1]{3,2,1,0:T(8,128)S(1)} %get-tuple-element.68), channel_id=1, source_target_pairs={{0,4},{4,8},{8,12},{1,5},{5,9},{9,13},{2,6},{6,10},{10,14},{3,7},{... | collective-permute-start | bytes 776 | tf_op jit(solution)/shard_map/ppermute | solution.py:17
  26.7 7.4 %collective-permute-start.13 = (f32[1,8,8,1]{3,2,1,0:T(8,128)S(1)}, f32[1,8,8,1]{3,2,1,0:T(8,128)S(1)}, u32[]{:S(2)}, u32[]{:S(2)}) collective-permute-start(f32[1,8,8,1]{3,2,1,0:T(8,128)S(1)} %get-tuple-element.69), channel_id=1, source_target_pairs={{4,0},{8,4},{12,8},{5,1},{9,5},{13,9},{6,2},{10,6},{14,10},{7,3},{... | collective-permute-start | bytes 776 | tf_op jit(solution)/shard_map/ppermute | solution.py:19
  28.2 10.8 %collective-permute-start.2 = (f32[2,10,16,1]{3,2,1,0:T(8,128)S(1)}, f32[2,10,16,1]{3,2,1,0:T(8,128)S(1)}, u32[]{:S(2)}, u32[]{:S(2)}) collective-permute-start(f32[2,10,16,1]{3,2,1,0:T(8,128)S(1)} %get-tuple-element.37), channel_id=1, source_target_pairs={{0,4},{4,8},{8,12},{1,5},{5,9},{9,13},{2,6},{6,10},{10,14},{3,7},{... | collective-permute-start | bytes 3848 | tf_op jit(solution)/shard_map/ppermute | solution.py:17
  32.8 9.7 %collective-permute-start.3 = (f32[2,10,16,1]{3,2,1,0:T(8,128)S(1)}, f32[2,10,16,1]{3,2,1,0:T(8,128)S(1)}, u32[]{:S(2)}, u32[]{:S(2)}) collective-permute-start(f32[2,10,16,1]{3,2,1,0:T(8,128)S(1)} %get-tuple-element.38), channel_id=1, source_target_pairs={{4,0},{8,4},{12,8},{5,1},{9,5},{13,9},{6,2},{10,6},{14,10},{7,3},{... | collective-permute-start | bytes 3848 | tf_op jit(solution)/shard_map/ppermute | solution.py:19
  34.2 13.4 %collective-permute-start.14 = (f32[1,8,1,130]{3,2,1,0:T(1,128)S(1)}, f32[1,8,1,130]{3,2,1,0:T(1,128)S(1)}, u32[]{:S(2)}, u32[]{:S(2)}) collective-permute-start(f32[1,8,1,130]{3,2,1,0:T(1,128)S(1)} %get-tuple-element.60), channel_id=1, source_target_pairs={{0,1},{1,2},{2,3},{4,5},{5,6},{6,7},{8,9},{9,10},{10,11},{12,13},{... | collective-permute-start | bytes 12488 | tf_op jit(solution)/shard_map/ppermute | solution.py:17
  37.7 9.9 %collective-permute-start.15 = (f32[1,8,1,130]{3,2,1,0:T(1,128)S(1)}, f32[1,8,1,130]{3,2,1,0:T(1,128)S(1)}, u32[]{:S(2)}, u32[]{:S(2)}) collective-permute-start(f32[1,8,1,130]{3,2,1,0:T(1,128)S(1)} %get-tuple-element.61), channel_id=1, source_target_pairs={{1,0},{2,1},{3,2},{5,4},{6,5},{7,6},{9,8},{10,9},{11,10},{13,12},{... | collective-permute-start | bytes 12488 | tf_op jit(solution)/shard_map/ppermute | solution.py:19
  42.8 5.0 %collective-permute-start.4 = (f32[2,10,1,258]{3,0,2,1:T(2,128)S(1)}, f32[2,10,1,258]{3,0,2,1:T(2,128)S(1)}, u32[]{:S(2)}, u32[]{:S(2)}) collective-permute-start(f32[2,10,1,258]{3,0,2,1:T(2,128)S(1)} %copy.77), channel_id=1, source_target_pairs={{0,1},{1,2},{2,3},{4,5},{5,6},{6,7},{8,9},{9,10},{10,11},{12,13},{... | collective-permute-start | bytes 61928 | tf_op jit(solution)/shard_map/ppermute | solution.py:17
  46.3 5.8 %collective-permute-start.5 = (f32[2,10,1,258]{3,0,2,1:T(2,128)S(1)}, f32[2,10,1,258]{3,0,2,1:T(2,128)S(1)}, u32[]{:S(2)}, u32[]{:S(2)}) collective-permute-start(f32[2,10,1,258]{3,0,2,1:T(2,128)S(1)} %copy.78), channel_id=1, source_target_pairs={{1,0},{2,1},{3,2},{5,4},{6,5},{7,6},{9,8},{10,9},{11,10},{13,12},{... | collective-permute-start | bytes 61928 | tf_op jit(solution)/shard_map/ppermute | solution.py:19
  68.9 4.5 %collective-permute-start.16 = (f32[1,8,8,1]{3,2,1,0:T(8,128)S(1)}, f32[1,8,8,1]{3,2,1,0:T(8,128)S(1)}, u32[]{:S(2)}, u32[]{:S(2)}) collective-permute-start(f32[1,8,8,1]{3,2,1,0:T(8,128)S(1)} %get-tuple-element.66), channel_id=1, source_target_pairs={{0,4},{4,8},{8,12},{1,5},{5,9},{9,13},{2,6},{6,10},{10,14},{3,7},{... | collective-permute-start | bytes 776 | tf_op jit(solution)/shard_map/ppermute | solution.py:17
  71.8 6.3 %collective-permute-start.17 = (f32[1,8,8,1]{3,2,1,0:T(8,128)S(1)}, f32[1,8,8,1]{3,2,1,0:T(8,128)S(1)}, u32[]{:S(2)}, u32[]{:S(2)}) collective-permute-start(f32[1,8,8,1]{3,2,1,0:T(8,128)S(1)} %get-tuple-element.67), channel_id=1, source_target_pairs={{4,0},{8,4},{12,8},{5,1},{9,5},{13,9},{6,2},{10,6},{14,10},{7,3},{... | collective-permute-start | bytes 776 | tf_op jit(solution)/shard_map/ppermute | solution.py:19
  78.2 4.8 %collective-permute-start.18 = (f32[1,8,1,130]{3,2,1,0:T(1,128)S(1)}, f32[1,8,1,130]{3,2,1,0:T(1,128)S(1)}, u32[]{:S(2)}, u32[]{:S(2)}) collective-permute-start(f32[1,8,1,130]{3,2,1,0:T(1,128)S(1)} %get-tuple-element.58), channel_id=1, source_target_pairs={{0,1},{1,2},{2,3},{4,5},{5,6},{6,7},{8,9},{9,10},{10,11},{12,13},{... | collective-permute-start | bytes 12488 | tf_op jit(solution)/shard_map/ppermute | solution.py:17
  81.7 5.5 %collective-permute-start.19 = (f32[1,8,1,130]{3,2,1,0:T(1,128)S(1)}, f32[1,8,1,130]{3,2,1,0:T(1,128)S(1)}, u32[]{:S(2)}, u32[]{:S(2)}) collective-permute-start(f32[1,8,1,130]{3,2,1,0:T(1,128)S(1)} %get-tuple-element.59), channel_id=1, source_target_pairs={{1,0},{2,1},{3,2},{5,4},{6,5},{7,6},{9,8},{10,9},{11,10},{13,12},{... | collective-permute-start | bytes 12488 | tf_op jit(solution)/shard_map/ppermute | solution.py:19
  87.6 6.4 %collective-permute-start.20 = (f32[1,8,8,1]{3,2,1,0:T(8,128)S(1)}, f32[1,8,8,1]{3,2,1,0:T(8,128)S(1)}, u32[]{:S(2)}, u32[]{:S(2)}) collective-permute-start(f32[1,8,8,1]{3,2,1,0:T(8,128)S(1)} %get-tuple-element.64), channel_id=1, source_target_pairs={{0,4},{4,8},{8,12},{1,5},{5,9},{9,13},{2,6},{6,10},{10,14},{3,7},{... | collective-permute-start | bytes 776 | tf_op jit(solution)/shard_map/ppermute | solution.py:17
  92.4 5.8 %collective-permute-start.21 = (f32[1,8,8,1]{3,2,1,0:T(8,128)S(1)}, f32[1,8,8,1]{3,2,1,0:T(8,128)S(1)}, u32[]{:S(2)}, u32[]{:S(2)}) collective-permute-start(f32[1,8,8,1]{3,2,1,0:T(8,128)S(1)} %get-tuple-element.65), channel_id=1, source_target_pairs={{4,0},{8,4},{12,8},{5,1},{9,5},{13,9},{6,2},{10,6},{14,10},{7,3},{... | collective-permute-start | bytes 776 | tf_op jit(solution)/shard_map/ppermute | solution.py:19
  98.3 7.4 %collective-permute-start.22 = (f32[1,8,1,130]{3,2,1,0:T(1,128)S(1)}, f32[1,8,1,130]{3,2,1,0:T(1,128)S(1)}, u32[]{:S(2)}, u32[]{:S(2)}) collective-permute-start(f32[1,8,1,130]{3,2,1,0:T(1,128)S(1)} %get-tuple-element.56), channel_id=1, source_target_pairs={{0,1},{1,2},{2,3},{4,5},{5,6},{6,7},{8,9},{9,10},{10,11},{12,13},{... | collective-permute-start | bytes 12488 | tf_op jit(solution)/shard_map/ppermute | solution.py:17
  101.8 5.5 %collective-permute-start.23 = (f32[1,8,1,130]{3,2,1,0:T(1,128)S(1)}, f32[1,8,1,130]{3,2,1,0:T(1,128)S(1)}, u32[]{:S(2)}, u32[]{:S(2)}) collective-permute-start(f32[1,8,1,130]{3,2,1,0:T(1,128)S(1)} %get-tuple-element.57), channel_id=1, source_target_pairs={{1,0},{2,1},{3,2},{5,4},{6,5},{7,6},{9,8},{10,9},{11,10},{13,12},{... | collective-permute-start | bytes 12488 | tf_op jit(solution)/shard_map/ppermute | solution.py:19
  103.1 4.5 %collective-permute-start.6 = (f32[1,1,16,256]{3,2,1,0:T(8,128)S(1)}, f32[1,1,16,256]{3,2,1,0:T(8,128)S(1)}, u32[]{:S(2)}, u32[]{:S(2)}) collective-permute-start(f32[1,1,16,256]{3,2,1,0:T(8,128)S(1)} %get-tuple-element.52), channel_id=1, source_target_pairs={{0,16},{1,17},{2,18},{3,19},{4,20},{5,21},{6,22},{7,23},{8,24},{9,... | collective-permute-start | bytes 49160 | tf_op jit(solution)/shard_map/ppermute | solution.py:17
  104.4 3.2 %collective-permute-start.7 = (f32[1,1,16,256]{3,2,1,0:T(8,128)S(1)}, f32[1,1,16,256]{3,2,1,0:T(8,128)S(1)}, u32[]{:S(2)}, u32[]{:S(2)}) collective-permute-start(f32[1,1,16,256]{3,2,1,0:T(8,128)S(1)} %get-tuple-element.53), channel_id=1, source_target_pairs={{16,0},{17,1},{18,2},{19,3},{20,4},{21,5},{22,6},{23,7},{24,8},{25... | collective-permute-start | bytes 49160 | tf_op jit(solution)/shard_map/ppermute | solution.py:19
  107.7 10.1 %collective-permute-start.8 = (f32[1,10,16,1]{3,2,1,0:T(8,128)S(1)}, f32[1,10,16,1]{3,2,1,0:T(8,128)S(1)}, u32[]{:S(2)}, u32[]{:S(2)}) collective-permute-start(f32[1,10,16,1]{3,2,1,0:T(8,128)S(1)} %get-tuple-element.45), channel_id=1, source_target_pairs={{0,4},{4,8},{8,12},{1,5},{5,9},{9,13},{2,6},{6,10},{10,14},{3,7},{... | collective-permute-start | bytes 1928 | tf_op jit(solution)/shard_map/ppermute | solution.py:17
  110.6 7.2 %collective-permute-start.9 = (f32[1,10,16,1]{3,2,1,0:T(8,128)S(1)}, f32[1,10,16,1]{3,2,1,0:T(8,128)S(1)}, u32[]{:S(2)}, u32[]{:S(2)}) collective-permute-start(f32[1,10,16,1]{3,2,1,0:T(8,128)S(1)} %get-tuple-element.46), channel_id=1, source_target_pairs={{4,0},{8,4},{12,8},{5,1},{9,5},{13,9},{6,2},{10,6},{14,10},{7,3},{... | collective-permute-start | bytes 1928 | tf_op jit(solution)/shard_map/ppermute | solution.py:19
  111.9 11.7 %collective-permute-start.24 = (f32[1,8,8,1]{3,2,1,0:T(8,128)S(1)}, f32[1,8,8,1]{3,2,1,0:T(8,128)S(1)}, u32[]{:S(2)}, u32[]{:S(2)}) collective-permute-start(f32[1,8,8,1]{3,2,1,0:T(8,128)S(1)} %get-tuple-element.62), channel_id=1, source_target_pairs={{0,4},{4,8},{8,12},{1,5},{5,9},{9,13},{2,6},{6,10},{10,14},{3,7},{... | collective-permute-start | bytes 776 | tf_op jit(solution)/shard_map/ppermute | solution.py:17
  116.5 7.2 %collective-permute-start.25 = (f32[1,8,8,1]{3,2,1,0:T(8,128)S(1)}, f32[1,8,8,1]{3,2,1,0:T(8,128)S(1)}, u32[]{:S(2)}, u32[]{:S(2)}) collective-permute-start(f32[1,8,8,1]{3,2,1,0:T(8,128)S(1)} %get-tuple-element.63), channel_id=1, source_target_pairs={{4,0},{8,4},{12,8},{5,1},{9,5},{13,9},{6,2},{10,6},{14,10},{7,3},{... | collective-permute-start | bytes 776 | tf_op jit(solution)/shard_map/ppermute | solution.py:19
  118.0 11.7 %collective-permute-start.10 = (f32[1,10,1,258]{3,2,1,0:T(1,128)S(1)}, f32[1,10,1,258]{3,2,1,0:T(1,128)S(1)}, u32[]{:S(2)}, u32[]{:S(2)}) collective-permute-start(f32[1,10,1,258]{3,2,1,0:T(1,128)S(1)} %get-tuple-element.35), channel_id=1, source_target_pairs={{0,1},{1,2},{2,3},{4,5},{5,6},{6,7},{8,9},{9,10},{10,11},{12,13},{... | collective-permute-start | bytes 30968 | tf_op jit(solution)/shard_map/ppermute | solution.py:17
  122.4 7.3 %collective-permute-start.11 = (f32[1,10,1,258]{3,2,1,0:T(1,128)S(1)}, f32[1,10,1,258]{3,2,1,0:T(1,128)S(1)}, u32[]{:S(2)}, u32[]{:S(2)}) collective-permute-start(f32[1,10,1,258]{3,2,1,0:T(1,128)S(1)} %get-tuple-element.36), channel_id=1, source_target_pairs={{1,0},{2,1},{3,2},{5,4},{6,5},{7,6},{9,8},{10,9},{11,10},{13,12},{... | collective-permute-start | bytes 30968 | tf_op jit(solution)/shard_map/ppermute | solution.py:19
  123.8 9.0 %collective-permute-start.26 = (f32[1,8,1,130]{3,2,1,0:T(1,128)S(1)}, f32[1,8,1,130]{3,2,1,0:T(1,128)S(1)}, u32[]{:S(2)}, u32[]{:S(2)}) collective-permute-start(f32[1,8,1,130]{3,2,1,0:T(1,128)S(1)} %get-tuple-element.54), channel_id=1, source_target_pairs={{0,1},{1,2},{2,3},{4,5},{5,6},{6,7},{8,9},{9,10},{10,11},{12,13},{... | collective-permute-start | bytes 12488 | tf_op jit(solution)/shard_map/ppermute | solution.py:17
  128.4 5.5 %collective-permute-start.27 = (f32[1,8,1,130]{3,2,1,0:T(1,128)S(1)}, f32[1,8,1,130]{3,2,1,0:T(1,128)S(1)}, u32[]{:S(2)}, u32[]{:S(2)}) collective-permute-start(f32[1,8,1,130]{3,2,1,0:T(1,128)S(1)} %get-tuple-element.55), channel_id=1, source_target_pairs={{1,0},{2,1},{3,2},{5,4},{6,5},{7,6},{9,8},{10,9},{11,10},{13,12},{... | collective-permute-start | bytes 12488 | tf_op jit(solution)/shard_map/ppermute | solution.py:19
  130.2 3.8 %collective-permute-start.28 = (f32[1,1,16,256]{3,2,1,0:T(8,128)S(1)}, f32[1,1,16,256]{3,2,1,0:T(8,128)S(1)}, u32[]{:S(2)}, u32[]{:S(2)}) collective-permute-start(f32[1,1,16,256]{3,2,1,0:T(8,128)S(1)} %get-tuple-element.50), channel_id=1, source_target_pairs={{0,16},{1,17},{2,18},{3,19},{4,20},{5,21},{6,22},{7,23},{8,24},{9,... | collective-permute-start | bytes 49160 | tf_op jit(solution)/shard_map/ppermute | solution.py:17
  131.5 3.1 %collective-permute-start.29 = (f32[1,1,16,256]{3,2,1,0:T(8,128)S(1)}, f32[1,1,16,256]{3,2,1,0:T(8,128)S(1)}, u32[]{:S(2)}, u32[]{:S(2)}) collective-permute-start(f32[1,1,16,256]{3,2,1,0:T(8,128)S(1)} %get-tuple-element.51), channel_id=1, source_target_pairs={{16,0},{17,1},{18,2},{19,3},{20,4},{21,5},{22,6},{23,7},{24,8},{25... | collective-permute-start | bytes 49160 | tf_op jit(solution)/shard_map/ppermute | solution.py:19
  134.7 6.6 %collective-permute-start.30 = (f32[1,10,16,1]{3,2,1,0:T(8,128)S(1)}, f32[1,10,16,1]{3,2,1,0:T(8,128)S(1)}, u32[]{:S(2)}, u32[]{:S(2)}) collective-permute-start(f32[1,10,16,1]{3,2,1,0:T(8,128)S(1)} %get-tuple-element.43), channel_id=1, source_target_pairs={{0,4},{4,8},{8,12},{1,5},{5,9},{9,13},{2,6},{6,10},{10,14},{3,7},{... | collective-permute-start | bytes 1928 | tf_op jit(solution)/shard_map/ppermute | solution.py:17
  139.3 6.3 %collective-permute-start.31 = (f32[1,10,16,1]{3,2,1,0:T(8,128)S(1)}, f32[1,10,16,1]{3,2,1,0:T(8,128)S(1)}, u32[]{:S(2)}, u32[]{:S(2)}) collective-permute-start(f32[1,10,16,1]{3,2,1,0:T(8,128)S(1)} %get-tuple-element.44), channel_id=1, source_target_pairs={{4,0},{8,4},{12,8},{5,1},{9,5},{13,9},{6,2},{10,6},{14,10},{7,3},{... | collective-permute-start | bytes 1928 | tf_op jit(solution)/shard_map/ppermute | solution.py:19
  145.8 6.6 %collective-permute-start.32 = (f32[1,10,1,258]{3,2,1,0:T(1,128)S(1)}, f32[1,10,1,258]{3,2,1,0:T(1,128)S(1)}, u32[]{:S(2)}, u32[]{:S(2)}) collective-permute-start(f32[1,10,1,258]{3,2,1,0:T(1,128)S(1)} %get-tuple-element.33), channel_id=1, source_target_pairs={{0,1},{1,2},{2,3},{4,5},{5,6},{6,7},{8,9},{9,10},{10,11},{12,13},{... | collective-permute-start | bytes 30968 | tf_op jit(solution)/shard_map/ppermute | solution.py:17
  150.3 5.6 %collective-permute-start.33 = (f32[1,10,1,258]{3,2,1,0:T(1,128)S(1)}, f32[1,10,1,258]{3,2,1,0:T(1,128)S(1)}, u32[]{:S(2)}, u32[]{:S(2)}) collective-permute-start(f32[1,10,1,258]{3,2,1,0:T(1,128)S(1)} %get-tuple-element.34), channel_id=1, source_target_pairs={{1,0},{2,1},{3,2},{5,4},{6,5},{7,6},{9,8},{10,9},{11,10},{13,12},{... | collective-permute-start | bytes 30968 | tf_op jit(solution)/shard_map/ppermute | solution.py:19
where the time goes:
time: 158 us; the launch traced here: 157 us
  starting transfers between devices  82.9 us (52%)
  waiting for transfers between devices  33.3 us (21%)
  local copies, waits for them, and re-layouts  21.7 us (14%)
  other arithmetic  13.4 us (8%)
  blocking collectives  4.45 us (3%)
    ppermute x17, starting transfers between devices, padded_2(): lax.ppermute(tail, axis, [(i, (i + 1) % count) for i in range(ends)])  60.8 us
    ppermute x17, waiting for transfers between devices, padded_2(): lax.ppermute(head, axis, [((i + 1) % count, i) for i in range(ends)])  31.9 us
    ppermute x17, starting transfers between devices, padded_2(): lax.ppermute(head, axis, [((i + 1) % count, i) for i in range(ends)])  22.1 us
    reshape x2, local copies, waits for them, and re-layouts, restrict(): return field.reshape(a // 2, 2, b // 2, 2, c // 2, 2).mean(axis=(1, 3, 5))  20.3 us
    reduce_sum x2, other arithmetic, restrict(): return field.reshape(a // 2, 2, b // 2, 2, c // 2, 2).mean(axis=(1, 3, 5))  8.07 us
  transfers between devices with their start and end apart: 34, of which 14 were waited for; matrix products, arithmetic and copies ran while one was open for 11% of the time, Pallas kernels for 0%

commit v1 on v0

v1 whole, which is shorter than its diff:
```python
import functools

import jax
import jax.numpy as jnp
from jax import lax
from jax.experimental import pallas as pl
from jax.experimental.pallas import tpu as pltpu
from jax.sharding import PartitionSpec as P

KSWEEP = 4
MESH = pl.DeviceIdType.MESH
AXES = ("pencil", "coarse", "gz")
LANES = 128

THETA = 1.1
DELTA = 0.8
SIGMA = THETA / DELTA
RHO0 = 1.0 / SIGMA
RHO1 = 1.0 / (2.0 * SIGMA - RHO0)


def back(v, step, axis):
    return pltpu.roll(v, step, axis)


def ahead(v, step, axis):
    return pltpu.roll(v, v.shape[axis] - step, axis)


def local_operate(v, cx, cy, cz, step):
    gx = cx * (v[1:] - v[:-1])
    zero = jnp.zeros_like(v[:1])
    gy = cy * (v - back(v, step, 1))
    gz = cz * (v - back(v, step, 2))
    return (
        (gy - ahead(gy, step, 1))
        + (gz - ahead(gz, step, 2))
        + (jnp.concatenate([zero, gx], 0) - jnp.concatenate([gx, zero], 0))
    )


def with_ends(inner, low, high):
    return jnp.concatenate([inner[:1] + low, inner[1:-1], inner[-1:] + high], 0)


def y_halo(low, high, shape):
    n, y, z = shape
    half = (n, y // 2, z)
    return jnp.concatenate(
        [jnp.broadcast_to(low[:, None, :], half), jnp.broadcast_to(high[:, None, :], half)], 1
    )


def z_halo(low, high, first, shape):
    n, y, z = shape
    out = []
    for i in range(n):
        at = slice(first + i, first + i + 1)
        out.append(
            jnp.concatenate(
                [
                    jnp.broadcast_to(low[:, at], (y, z // 2)),
                    jnp.broadcast_to(high[:, at], (y, z // 2)),
                ],
                1,
            )
        )
    return jnp.stack(out, 0)


def z_pack(fields, side):
    slot = 0
    lane = lax.broadcasted_iota(jnp.int32, (fields[0].shape[1], LANES), 1)
    packed = jnp.zeros(lane.shape, jnp.float32)
    for v in fields:
        tile = v[:, :, :LANES] if side == 0 else v[:, :, v.shape[2] - LANES :]
        for i in range(v.shape[0]):
            shift = (slot + side) % LANES
            moved = pltpu.roll(tile[i], shift, 1) if shift else tile[i]
            packed = jnp.where(lane == slot, moved, packed)
            slot += 1
    return packed


def pair_sums(v, row_even, lane_even):
    n, y, z = v.shape
    s = v.reshape(n // 2, 2, y, z)
    s = s[:, 0] + s[:, 1]
    s = s + jnp.where(row_even, ahead(s, 1, 1), back(s, 1, 1))
    return s + jnp.where(lane_even, ahead(s, 1, 2), back(s, 1, 2))


def kernel(
    sizes, f_hbm, k_hbm, u_hbm, new_hbm, smooth_hbm,
    f_ref, k_ref, u_ref, new_ref, smooth_ref,
    sxa, rxa, sya, rya, sza, rza,
    d_ref, rxf, syf, ryf, szf, rzf,
    e_ref, rxc, syc, ryc, szc, rzc,
    in_sem, out_sem, send_sem, recv_sem,
):
    nx, ny, nz = f_ref.shape
    hx = nx // 2
    sweeps = KSWEEP - 1
    at = [lax.axis_index(a) for a in AXES]
    has = []
    for dim in range(3):
        has += [at[dim] > 0, at[dim] < sizes[dim] - 1]

    def neighbour(d):
        return {AXES[d // 2]: at[d // 2] + (1 if d % 2 else -1)}

    barrier = pltpu.get_barrier_semaphore()
    for d in range(6):

        @pl.when(has[d])
        def _(d=d):
            pl.semaphore_signal(barrier, inc=1, device_id=neighbour(d), device_id_type=MESH)

    loads = [
        pltpu.make_async_copy(src, dst, in_sem.at[i])
        for i, (src, dst) in enumerate(((k_hbm, k_ref), (u_hbm, u_ref), (f_hbm, f_ref)))
    ]
    for c in loads:
        c.start()

    slots = {}
    slots[0] = [(rxa.at[0], rxa.at[1]), (rya.at[0], rya.at[1]), (rza.at[0], rza.at[1])]
    for j in range(2):
        slots[1 + j] = [(r.at[j, 0], r.at[j, 1]) for r in (rxf, ryf, rzf)]
    for j in range(sweeps):
        slots[3 + j] = [(r.at[j, 0], r.at[j, 1]) for r in (rxc, ryc, rzc)]
    for d in range(6):

        @pl.when(jnp.logical_not(has[d]))
        def _(d=d):
            for part in slots.values():
                ref = part[d // 2][d % 2]
                ref[...] = jnp.zeros(ref.shape, jnp.float32)

    def copy(part, d, src):
        return pltpu.make_async_remote_copy(
            src_ref=src,
            dst_ref=slots[part][d // 2][1 - d % 2],
            send_sem=send_sem.at[part, d],
            recv_sem=recv_sem.at[part, 1 - d % 2 + 2 * (d // 2)],
            device_id=neighbour(d),
            device_id_type=MESH,
        )

    started = []

    def send(part, d, src):
        @pl.when(has[d])
        def _():
            copy(part, d, src).start()

        started.append((part, d, src))

    def receive(part, d, src):
        @pl.when(has[d])
        def _():
            pltpu.make_async_remote_copy(
                src_ref=src,
                dst_ref=slots[part][d // 2][d % 2],
                send_sem=send_sem.at[part, d],
                recv_sem=recv_sem.at[part, d],
                device_id=neighbour(d),
                device_id_type=MESH,
            ).wait_recv()

    lane = lax.broadcasted_iota(jnp.int32, (1, ny, nz), 2)
    row = lax.broadcasted_iota(jnp.int32, (1, ny, nz), 1)
    lane_even, row_even = lane % 2 == 0, row % 2 == 0

    loads[0].wait()
    loads[1].wait()
    k = k_ref[...]
    u = u_ref[...]
    kc = pair_sums(k, row_even, lane_even) * 0.125
    for s in range(2):
        x = -1 if s else 0
        sxa[s, 0] = u[x]
        sxa[s, 1] = k[x]
        sxa[s, 2] = kc[x]
        y = ny - 1 if s else 0
        sya[s, 0:nx] = u_ref[:, y, :]
        sya[s, nx : 2 * nx] = k_ref[:, y, :]
        sya[s, 2 * nx : 2 * nx + hx] = kc[:, y, :]
        sza[s] = z_pack([u, k, kc], s)
    pl.semaphore_wait(barrier, sum(h.astype(jnp.int32) for h in has))
    for d in range(6):
        send(0, d, (sxa, sya, sza)[d // 2].at[d % 2])

    def coefficients(k, step, scale):
        cx = scale * (k[1:] + k[:-1])
        cy = jnp.where(row < step, 0.0, scale * (k + back(k, step, 1)))
        cz = jnp.where(lane < step, 0.0, scale * (k + back(k, step, 2)))
        zero = jnp.zeros_like(k[:1])
        diag = (
            (cy + ahead(cy, step, 1))
            + (cz + ahead(cz, step, 2))
            + (jnp.concatenate([zero, cx], 0) + jnp.concatenate([cx, zero], 0))
        )
        return cx, cy, cz, diag

    def end_coefficients(k, halo, step, scale):
        xl, xh, hy, hz = halo
        bx = scale * (k[:1] + xl), scale * (k[-1:] + xh)
        by = jnp.where((row < step) | (row >= ny - step), scale * (k + hy), 0.0)
        bz = jnp.where((lane < step) | (lane >= nz - step), scale * (k + hz), 0.0)
        return bx, by, bz

    def end_operate(local, v, halo, ends):
        xl, xh, hy, hz = halo
        bx, by, bz = ends
        both = local + by * (v - hy) + bz * (v - hz)
        return with_ends(both, bx[0] * (v[:1] - xl), bx[1] * (v[-1:] - xh))

    cx, cy, cz, diag = coefficients(k, 1, 0.5)
    local_u = local_operate(u, cx, cy, cz, 1)
    ex, ey, ez, ediag = coefficients(kc, 2, 0.125)

    for d in range(6):
        receive(0, d, (sxa, sya, sza)[d // 2].at[d % 2])

    def first_halo(field, n):
        return (
            rxa[0, field][None],
            rxa[1, field][None],
            y_halo(rya[0, field * nx : field * nx + n], rya[1, field * nx : field * nx + n], (n, ny, nz)),
            z_halo(rza[0], rza[1], field * nx, (n, ny, nz)),
        )

    ends = end_coefficients(k, first_halo(1, nx), 1, 0.5)
    diag = with_ends(diag + ends[1] + ends[2], ends[0][0], ends[0][1])
    loads[2].wait()
    r0 = f_ref[...] - end_operate(local_u, u, first_halo(0, nx), ends)

    eends = end_coefficients(kc, first_halo(2, hx), 2, 0.125)
    ediag = with_ends(ediag + eends[1] + eends[2], eends[0][0], eends[0][1])
    einv = 0.8 / ediag
    rc = pair_sums(r0, row_even, lane_even) * 0.125
    ec = rc * einv

    def send_faces(part, v, own, sy, sz, ends):
        own[...] = v
        send(part, 0, own.at[0])
        send(part, 1, own.at[v.shape[0] - 1])
        for s in range(2):
            sy[s] = own[:, ny - 1 if s else 0, :]
            send(part, 2 + s, sy.at[s])
        for s in range(2):
            sz[s] = z_pack([v], s)
            send(part, 4 + s, sz.at[s])

    def halo_of(part, n):
        for d in range(6):
            receive(part, d, slots[part][d // 2][d % 2])
        (xl, xh), (yl, yh), (zl, zh) = slots[part]
        return (
            xl[...][None],
            xh[...][None],
            y_halo(yl[...], yh[...], (n, ny, nz)),
            z_halo(zl[...], zh[...], 0, (n, ny, nz)),
        )

    def send_coarse(j, v):
        send_faces(3 + j, v, e_ref.at[j], syc.at[j], szc.at[j], None)

    def send_fine(j, v):
        send_faces(1 + j, v, d_ref.at[j], syf.at[j], szf.at[j], None)

    def sweep(j, ec, local):
        return ec + (rc - end_operate(local, ec, halo_of(3 + j, hx), eends)) * einv

    send_coarse(0, ec)
    inv = 1.0 / diag
    d0 = r0 * inv * (1.0 / THETA)
    send_fine(0, d0)
    local_e = local_operate(ec, ex, ey, ez, 2)
    local_d0 = local_operate(d0, cx, cy, cz, 1)

    ec = sweep(0, ec, local_e)
    send_coarse(1, ec)
    r1 = r0 - end_operate(local_d0, d0, halo_of(1, nx), ends)
    d1 = (RHO1 * RHO0) * d0 + (2.0 * RHO1 / DELTA) * r1 * inv
    send_fine(1, d1)
    local_e = local_operate(ec, ex, ey, ez, 2)
    local_d1 = local_operate(d1, cx, cy, cz, 1)
    base = u + d0 + d1

    for j in range(1, sweeps - 1):
        ec = sweep(j, ec, local_e)
        send_coarse(j + 1, ec)
        local_e = local_operate(ec, ex, ey, ez, 2)

    smooth_ref[...] = r1 - end_operate(local_d1, d1, halo_of(2, nx), ends)
    out_smooth = pltpu.make_async_copy(smooth_ref, smooth_hbm, out_sem.at[0])
    out_smooth.start()

    ec = sweep(sweeps - 1, ec, local_e)
    new = base.reshape(hx, 2, ny, nz) + ec[:, None]
    new_ref[...] = new.reshape(nx, ny, nz)
    out_new = pltpu.make_async_copy(new_ref, new_hbm, out_sem.at[1])
    out_new.start()

    for part, d, src in started:

        @pl.when(has[d])
        def _(part=part, d=d, src=src):
            copy(part, d, src).wait_send()

    out_smooth.wait()
    out_new.wait()


def on_device(sizes, right_side, conductivity, guess):
    nx, ny, nz = right_side.shape
    hx = nx // 2
    sweeps = KSWEEP - 1
    rows = 2 * nx + hx
    vmem = lambda *shape: pltpu.VMEM(shape, jnp.float32)
    block = jax.ShapeDtypeStruct((nx, ny, nz), jnp.float32)
    anywhere = pl.BlockSpec(memory_space=pl.ANY)
    return pl.pallas_call(
        functools.partial(kernel, sizes),
        out_shape=(block, block),
        in_specs=[anywhere] * 3,
        out_specs=(anywhere, anywhere),
        scratch_shapes=[
            *[vmem(nx, ny, nz)] * 5,
            *[vmem(2, 3, ny, nz)] * 2,
            *[vmem(2, rows, nz)] * 2,
            *[vmem(2, ny, LANES)] * 2,
            vmem(2, nx, ny, nz),
            vmem(2, 2, ny, nz),
            *[vmem(2, 2, nx, nz)] * 2,
            *[vmem(2, 2, ny, LANES)] * 2,
            vmem(sweeps, hx, ny, nz),
            vmem(sweeps, 2, ny, nz),
            *[vmem(sweeps, 2, hx, nz)] * 2,
            *[vmem(sweeps, 2, ny, LANES)] * 2,
            pltpu.SemaphoreType.DMA((3,)),
            pltpu.SemaphoreType.DMA((2,)),
            pltpu.SemaphoreType.DMA((3 + sweeps, 6)),
            pltpu.SemaphoreType.DMA((3 + sweeps, 6)),
        ],
        compiler_params=pltpu.CompilerParams(
            collective_id=0, has_side_effects=True, vmem_limit_bytes=32 * 1024 * 1024
        ),
        cost_estimate=pl.CostEstimate(
            flops=150 * nx * ny * nz, bytes_accessed=20 * nx * ny * nz, transcendentals=0
        ),
    )(right_side, conductivity, guess)


def solution(mesh):
    spec = P("pencil", "coarse", "gz")
    return jax.shard_map(
        functools.partial(on_device, tuple(mesh.shape[a] for a in AXES)),
        mesh=mesh,
        in_specs=(spec, spec, spec),
        out_specs=(spec, spec),
        check_vma=False,
    )
```

time: 158 us -> 22.7 us (0.14)
  starting transfers between devices: 82.9 us -> 0 us
  waiting for transfers between devices: 33.3 us -> 0 us
  Pallas kernels: 0 us -> 17.8 us
  local copies, waits for them, and re-layouts: 21.7 us -> 4.02 us
  other arithmetic: 13.4 us -> 0 us
  blocking collectives: 4.45 us -> 0 us
    ppermute x34 -> x0, starting transfers between devices: 82.9 us -> none  [the longest x17 60.8 us: padded_2(): lax.ppermute(tail, axis, [(i, (i + 1) % count) for i in range(ends)])]
    ppermute x34 -> x0, waiting for transfers between devices: 33.3 us -> none  [the longest x17 31.9 us: padded_2(): lax.ppermute(head, axis, [((i + 1) % count, i) for i in range(ends)])]
    reshape x4 -> x0, local copies, waits for them, and re-layouts: 20.9 us -> none  [the longest x2 20.3 us: restrict(): return field.reshape(a // 2, 2, b // 2, 2, c // 2, 2).mean(axis=(1, 3, 5))]
    pallas_call x0 -> x1, Pallas kernels: none -> 17.8 us  [on_device(): pl.pallas_call(functools.partial(kernel, sizes), out_shape=(block, block)...]
    reduce_sum x2 -> x0, other arithmetic: 8.07 us -> none  [restrict(): return field.reshape(a // 2, 2, b // 2, 2, c // 2, 2).mean(axis=(1, 3, 5))]
    all_gather x2 -> x0, blocking collectives: 4.45 us -> none  [the longest x1 2.62 us: on_device(): lax.all_gather(coarse_k, 'pencil', axis=0, tiled=True)]
    unnamed x8, local copies, waits for them, and re-layouts: 0.05 us -> 4.02 us
    slice x8 -> x0, other arithmetic: 1.78 us -> none  [padded_2(): lax.slice_in_dim(cells, cells.shape[dim] - width, cells.shape[dim], axis=...]
  transfers between devices with their start and end apart: 34 -> 0, of which waited for: 14 -> 0; matrix products, arithmetic and copies ran while one was open for 11% -> 0% of each run, Pallas kernels for 0% -> 0%
where the time goes in v1:
time: 22.7 us; the launch traced here: 22.5 us
  Pallas kernels  17.8 us (78%)
  local copies, waits for them, and re-layouts  4.02 us (18%)
  between operations  0.65 us (3%)
    pallas_call x1, Pallas kernels, on_device(): pl.pallas_call(functools.partial(kernel, sizes), out_shape=(block, block)...  17.8 us
    unnamed x8, local copies, waits for them, and re-layouts  4.02 us

profile of v1, /device:TPU:0, one launch (start us, length us, event | category | flops | bytes accessed | tf_op | source)
XLA Modules:
  0.0 22.5 jit_solution(7889917547969667556)
XLA Ops:
  0.6 0.0 copy-start
  0.6 0.9 %copy-done = f32[8,16,256]{2,1,0:T(8,128)S(1)} copy-done((f32[8,16,256]{2,1,0:T(8,128)S(1)}, f32[8,16,256]{2,1,0:T(8,128)}, u32[]{:S(2)}) %copy-start) | copy-done | bytes 131096
  1.5 0.0 copy-start.1
  1.5 0.9 %copy-done.1 = f32[8,16,256]{2,1,0:T(8,128)S(1)} copy-done((f32[8,16,256]{2,1,0:T(8,128)S(1)}, f32[8,16,256]{2,1,0:T(8,128)}, u32[]{:S(2)}) %copy-start.1) | copy-done | bytes 131096
  2.4 0.0 copy-start.2
  2.4 0.9 %copy-done.2 = f32[8,16,256]{2,1,0:T(8,128)S(1)} copy-done((f32[8,16,256]{2,1,0:T(8,128)S(1)}, f32[8,16,256]{2,1,0:T(8,128)}, u32[]{:S(2)}) %copy-start.2) | copy-done | bytes 131096
  3.3 17.8 %shard_map.50 = (f32[8,16,256]{2,1,0:T(8,128)S(1)}, f32[8,16,256]{2,1,0:T(8,128)S(1)}) custom-call(f32[8,16,256]{2,1,0:T(8,128)S(1)} %copy-done, f32[8,16,256]{2,1,0:T(8,128)S(1)} %copy-done.1, f32[8,16,256]{2,1,0:T(8,128)S(1)} %copy-done.2), custom_call_target="tpu_custom_call" | custom-call | flops 4915200 | bytes 655360 | tf_op jit(solution)/shard_map/pallas_call | solution.py:325
  21.2 0.7 %copy.7 = f32[8,16,256]{2,1,0:T(8,128)} copy(f32[8,16,256]{2,1,0:T(8,128)S(1)} %get-tuple-element.4) | data formatting | bytes 262144
  21.8 0.7 %copy.8 = f32[8,16,256]{2,1,0:T(8,128)} copy(f32[8,16,256]{2,1,0:T(8,128)S(1)} %get-tuple-element.5) | data formatting | bytes 262144
Async XLA Ops:
  0.6 0.9 %copy-start = (f32[8,16,256]{2,1,0:T(8,128)S(1)}, f32[8,16,256]{2,1,0:T(8,128)}, u32[]{:S(2)}) copy-start(f32[8,16,256]{2,1,0:T(8,128)} %f_hbm.1) | copy-start | bytes 393220
  1.5 0.9 %copy-start.1 = (f32[8,16,256]{2,1,0:T(8,128)S(1)}, f32[8,16,256]{2,1,0:T(8,128)}, u32[]{:S(2)}) copy-start(f32[8,16,256]{2,1,0:T(8,128)} %k_hbm.1) | copy-start | bytes 393220
  2.4 0.9 %copy-start.2 = (f32[8,16,256]{2,1,0:T(8,128)S(1)}, f32[8,16,256]{2,1,0:T(8,128)}, u32[]{:S(2)}) copy-start(f32[8,16,256]{2,1,0:T(8,128)} %u_hbm.1) | copy-start | bytes 393220

commit v2 on v1

v2 whole, which is shorter than its diff:
```python
import functools

import jax
import jax.numpy as jnp
from jax import lax
from jax.experimental import pallas as pl
from jax.experimental.pallas import tpu as pltpu
from jax.sharding import PartitionSpec as P

KSWEEP = 4
MESH = pl.DeviceIdType.MESH
AXES = ("pencil", "coarse", "gz")
LANES = 128

THETA = 1.1
DELTA = 0.8
SIGMA = THETA / DELTA
RHO0 = 1.0 / SIGMA
RHO1 = 1.0 / (2.0 * SIGMA - RHO0)


def back(v, step, axis):
    return pltpu.roll(v, step, axis)


def ahead(v, step, axis):
    return pltpu.roll(v, v.shape[axis] - step, axis)


def local_operate(v, cx, cy, cz, step):
    gx = cx * (v[1:] - v[:-1])
    zero = jnp.zeros_like(v[:1])
    gy = cy * (v - back(v, step, 1))
    gz = cz * (v - back(v, step, 2))
    return (
        (gy - ahead(gy, step, 1))
        + (gz - ahead(gz, step, 2))
        + (jnp.concatenate([zero, gx], 0) - jnp.concatenate([gx, zero], 0))
    )


def with_ends(inner, low, high):
    return jnp.concatenate([inner[:1] + low, inner[1:-1], inner[-1:] + high], 0)


def pair_sums(v, row_even, lane_even):
    n, y, z = v.shape
    s = v.reshape(n // 2, 2, y, z)
    s = s[:, 0] + s[:, 1]
    s = s + jnp.where(row_even, ahead(s, 1, 1), back(s, 1, 1))
    return s + jnp.where(lane_even, ahead(s, 1, 2), back(s, 1, 2))


def y_halo(low, high, shape):
    n, y, z = shape
    half = (n, y // 2, z)
    return jnp.concatenate(
        [jnp.broadcast_to(low[:, None, :], half), jnp.broadcast_to(high[:, None, :], half)], 1
    )


def z_halo(low, high, first, width, shape):
    n, y, z = shape
    out = []
    for i in range(n):
        a = first + i * width + width - 1
        b = first + i * width
        out.append(
            jnp.concatenate(
                [
                    jnp.broadcast_to(low[:, a : a + 1], (y, z // 2)),
                    jnp.broadcast_to(high[:, b : b + 1], (y, z // 2)),
                ],
                1,
            )
        )
    return jnp.stack(out, 0)


def turned(v, shift):
    shift = shift % v.shape[1]
    return pltpu.roll(v, shift, 1) if shift else v


def z_pack(fields, side):
    at = 0
    lane = lax.broadcasted_iota(jnp.int32, (fields[0][0].shape[1], LANES), 1)
    packed = jnp.zeros(lane.shape, jnp.float32)
    for v, width in fields:
        tile = v[:, :, :LANES] if side == 0 else v[:, :, v.shape[2] - LANES :]
        for i in range(v.shape[0]):
            moved = turned(tile[i], at + (width if side else 0))
            packed = jnp.where((lane >= at) & (lane < at + width), moved, packed)
            at += width
    return packed


def z_unpack(low, high, first, width, n):
    lane = lax.broadcasted_iota(jnp.int32, low.shape, 1)
    out = []
    for i in range(n):
        at = first + i * width
        a = jnp.where(lane < width, turned(high, -at), 0.0)
        out.append(jnp.where(lane >= LANES - width, turned(low, LANES - width - at), a))
    return jnp.stack(out, 0)


def tile_of(rows, shape):
    n, z = shape
    row = lax.broadcasted_iota(jnp.int32, (n, 8, z), 1)
    out = jnp.zeros((n, 8, z), jnp.float32)
    for (a, b), v in rows:
        out = jnp.where((row >= a) & (row < b), jnp.broadcast_to(v[:, None, :], out.shape), out)
    return out


def opposite(d):
    return tuple(-c for c in d)


X_WAYS = ((-1, 0, 0), (1, 0, 0))
Y_WAYS = ((0, -1, 0), (0, 1, 0))
Z_WAYS = ((0, 0, -1), (0, 0, 1))
YZ_WAYS = tuple((0, a, b) for a in (-1, 1) for b in (-1, 1))
AROUND = Y_WAYS + Z_WAYS + YZ_WAYS
FINE, COARSE = 2, KSWEEP - 1


def kernel(
    sizes, f_hbm, k_hbm, u_hbm, new_ref, smooth_ref,
    f_ref, k_ref, u_ref, kc_ref, d_ref, e_ref,
    sxa, rxa, sya, rya, sza, rza, rca,
    syb, ryb, szb, rzb, rcb,
    sxk, rxk, sxd, rxd, sxe, rxe,
    in_sem, send_sem, recv_sem,
):
    nx, ny, nz = f_ref.shape
    hx = nx // 2
    sweeps = KSWEEP - 1
    at = [lax.axis_index(a) for a in AXES]
    side = [{-1: at[i] > 0, 1: at[i] < sizes[i] - 1} for i in range(3)]

    def has(d):
        conditions = [side[i][c] for i, c in enumerate(d) if c]
        return functools.reduce(jnp.logical_and, conditions)

    def neighbour(d):
        return {AXES[i]: at[i] + c for i, c in enumerate(d) if c}

    partners = X_WAYS + AROUND
    barrier = pltpu.get_barrier_semaphore()
    for d in partners:

        @pl.when(has(d))
        def _(d=d):
            pl.semaphore_signal(barrier, inc=1, device_id=neighbour(d), device_id_type=MESH)

    loads = [
        pltpu.make_async_copy(src, dst, in_sem.at[i])
        for i, (src, dst) in enumerate(((k_hbm, k_ref), (u_hbm, u_ref), (f_hbm, f_ref)))
    ]
    for c in loads:
        c.start()

    def x_ways(s, r):
        return {d: (s.at[i], r.at[i]) for i, d in enumerate(X_WAYS)}

    def around(sy, ry, sz, rz, rc):
        out = {d: (sy.at[i], ry.at[i]) for i, d in enumerate(Y_WAYS)}
        out.update({d: (sz.at[i], rz.at[i]) for i, d in enumerate(Z_WAYS)})
        for i, d in enumerate(YZ_WAYS):
            rows = pl.ds(ny - 8 if d[1] > 0 else 0, 8)
            out[d] = (sz.at[1 if d[2] > 0 else 0, rows], rc.at[i])
        return out

    exchanges = {
        "first_x": x_ways(sxa, rxa),
        "first": around(sya, rya, sza, rza, rca),
        "second": around(syb, ryb, szb, rzb, rcb),
        "k": x_ways(sxk, rxk),
    }
    for i in range(2):
        exchanges["d", i] = x_ways(sxd.at[i], rxd.at[i])
    for i in range(sweeps):
        exchanges["e", i] = x_ways(sxe.at[i], rxe.at[i])
    number = {}
    for name, ways in exchanges.items():
        for d in ways:
            number[name, d] = len(number)

    for way in partners:

        @pl.when(jnp.logical_not(has(way)))
        def _(way=way):
            for ways in exchanges.values():
                if way in ways:
                    ref = ways[way][1]
                    ref[...] = jnp.zeros(ref.shape, jnp.float32)

    def copy(name, d):
        return pltpu.make_async_remote_copy(
            src_ref=exchanges[name][d][0],
            dst_ref=exchanges[name][opposite(d)][1],
            send_sem=send_sem.at[number[name, d]],
            recv_sem=recv_sem.at[number[name, opposite(d)]],
            device_id=neighbour(d),
            device_id_type=MESH,
        )

    def send(name):
        for d in exchanges[name]:

            @pl.when(has(d))
            def _(d=d):
                copy(name, d).start()

    def receive(name):
        for d in exchanges[name]:

            @pl.when(has(d))
            def _(d=d):
                pltpu.make_async_remote_copy(
                    src_ref=exchanges[name][d][0],
                    dst_ref=exchanges[name][d][1],
                    send_sem=send_sem.at[number[name, d]],
                    recv_sem=recv_sem.at[number[name, d]],
                    device_id=neighbour(d),
                    device_id_type=MESH,
                ).wait_recv()

    lane = lax.broadcasted_iota(jnp.int32, (1, ny, nz), 2)
    row = lax.broadcasted_iota(jnp.int32, (1, ny, nz), 1)
    lane_even, row_even = lane % 2 == 0, row % 2 == 0

    def put_rows(to, first, ref, depth, step, s):
        n = ref.shape[0]
        for r in range(depth):
            y = ny - 1 - r * step if s else r * step
            to[s, first + r * n : first + (r + 1) * n] = ref[:, y, :]
        return first + depth * n

    loads[0].wait()
    k = k_ref[...]
    kc = pair_sums(k, row_even, lane_even) * 0.125
    kc_ref[...] = kc
    loads[1].wait()
    u = u_ref[...]
    for s in range(2):
        x = -1 if s else 0
        sxa[s, 0] = u[x]
        sxa[s, 1] = k[x]
        sxa[s, 2] = kc[x]
        to = put_rows(sya, 0, u_ref, 1, 1, s)
        to = put_rows(sya, to, k_ref, FINE, 1, s)
        put_rows(sya, to, kc_ref, COARSE, 2, s)
        sza[s] = z_pack([(u, FINE), (k, FINE), (kc, 2 * COARSE)], s)
    pl.semaphore_wait(barrier, sum(has(d).astype(jnp.int32) for d in partners))
    send("first")
    send("first_x")

    def coefficients(k, step, scale, keep):
        cx = scale * (k[1:] + k[:-1])
        cy = scale * (k + back(k, step, 1))
        cz = scale * (k + back(k, step, 2))
        if keep is not None:
            cy = jnp.where(row < keep, 0.0, cy)
            cz = jnp.where(lane < keep, 0.0, cz)
        zero = jnp.zeros_like(k[:1])
        diag = (
            (cy + ahead(cy, step, 1))
            + (cz + ahead(cz, step, 2))
            + (jnp.concatenate([zero, cx], 0) + jnp.concatenate([cx, zero], 0))
        )
        return cx, cy, cz, diag

    def end_coefficients(k, halo, step, scale):
        xl, xh, hy, hz = halo
        bx = scale * (k[:1] + xl), scale * (k[-1:] + xh)
        by = jnp.where((row < step) | (row >= ny - step), scale * (k + hy), 0.0)
        bz = jnp.where((lane < step) | (lane >= nz - step), scale * (k + hz), 0.0)
        return bx, by, bz

    def end_operate(local, v, halo, ends):
        xl, xh, hy, hz = halo
        bx, by, bz = ends
        both = local + by * (v - hy) + bz * (v - hz)
        return with_ends(both, bx[0] * (v[:1] - xl), bx[1] * (v[-1:] - xh))

    cx, cy, cz, diag = coefficients(k, 1, 0.5, 1)
    local_u = local_operate(u, cx, cy, cz, 1)
    _, _, _, ediag = coefficients(kc, 2, 0.125, 2)

    receive("first_x")
    receive("first")

    def first_halo(field, first_row, first_lane, width, n):
        return (
            rxa[0, field][None],
            rxa[1, field][None],
            y_halo(rya[0, first_row : first_row + n], rya[1, first_row : first_row + n], (n, ny, nz)),
            z_halo(rza[0], rza[1], first_lane, width, (n, ny, nz)),
        )

    lane_k, lane_kc = FINE * nx, 2 * FINE * nx
    row_k, row_kc = nx, nx + FINE * nx
    ends = end_coefficients(k, first_halo(1, row_k, lane_k, FINE, nx), 1, 0.5)
    diag = with_ends(diag + ends[1] + ends[2], ends[0][0], ends[0][1])
    loads[2].wait()
    r0 = f_ref[...] - end_operate(local_u, u, first_halo(0, 0, 0, FINE, nx), ends)
    eends = end_coefficients(kc, first_halo(2, row_kc, lane_kc, 2 * COARSE, hx), 2, 0.125)
    ediag = with_ends(ediag + eends[1] + eends[2], eends[0][0], eends[0][1])
    e0 = pair_sums(r0, row_even, lane_even) * 0.125 * (0.8 / ediag)
    d0 = r0 * (1.0 / diag) * (1.0 / THETA)
    d_ref[...] = d0
    e_ref[...] = e0
    for s in range(2):
        to = put_rows(syb, 0, d_ref, FINE, 1, s)
        put_rows(syb, to, e_ref, COARSE, 2, s)
        szb[s] = z_pack([(d0, FINE), (e0, 2 * COARSE)], s)
    send("second")

    def wide_fine(v, ry, first_row, rz, rc, first_lane):
        def rows(i, r):
            return ry[i, first_row + r * nx : first_row + (r + 1) * nx]

        near = [((r, r + 1), rows(1, r)) for r in range(FINE)]
        near += [((7 - r, 8 - r), rows(0, r)) for r in range(FINE)]
        tall = jnp.concatenate([v, tile_of(near, (nx, nz))], 1)
        upper = lax.broadcasted_iota(jnp.int32, (8, LANES), 0) < 4
        ends = []
        for i in range(2):
            corner = jnp.where(upper, rc[2 + i], rc[i])
            ends.append(jnp.concatenate([rz[i], corner], 0))
        return jnp.concatenate([tall, z_unpack(ends[0], ends[1], first_lane, FINE, nx)], 2)

    def wide_coarse(v, ry, first_row, rz, rc, first_lane):
        def rows(i, r):
            return ry[i, first_row + r * hx : first_row + (r + 1) * hx]

        high = tile_of([((2 * r, 2 * r + 2), rows(1, r)) for r in range(COARSE)], (hx, nz))
        low = tile_of([((6 - 2 * r, 8 - 2 * r), rows(0, r)) for r in range(COARSE)], (hx, nz))
        tall = jnp.concatenate([v, high, low], 1)
        ends = [jnp.concatenate([rz[i], rc[2 + i], rc[i]], 0) for i in range(2)]
        return jnp.concatenate([tall, z_unpack(ends[0], ends[1], first_lane, 2 * COARSE, hx)], 2)

    wk = wide_fine(k, rya, row_k, rza, rca, lane_k)
    wkc = wide_coarse(kc, rya, row_kc, rza, rca, lane_kc)
    fine_rows = wk.shape[1]
    for s in range(2):
        x = -1 if s else 0
        sxk[s, :fine_rows] = wk[x]
        sxk[s, fine_rows:] = wkc[x]
    send("k")
    cx, cy, cz, diag = coefficients(wk, 1, 0.5, None)
    ex, ey, ez, ediag = coefficients(wkc, 2, 0.125, None)
    receive("k")
    bx = [0.5 * (wk[x][None] + rxk[s, :fine_rows][None]) for s, x in enumerate((0, -1))]
    be = [0.125 * (wkc[x][None] + rxk[s, fine_rows:][None]) for s, x in enumerate((0, -1))]
    diag = with_ends(diag, bx[0], bx[1])
    ediag = with_ends(ediag, be[0], be[1])
    inv = jnp.where(wk > 0.0, 1.0 / diag, 0.0)
    einv = jnp.where(wkc > 0.0, 0.8 / ediag, 0.0)

    def send_x(name, v):
        for i, d in enumerate(X_WAYS):
            exchanges[name][d][0][...] = v[-1 if i else 0]
        send(name)

    def operate(name, local, v, b):
        receive(name)
        low, high = [exchanges[name][d][1][...][None] for d in X_WAYS]
        return with_ends(local, b[0] * (v[:1] - low), b[1] * (v[-1:] - high))

    receive("second")
    e0 = wide_coarse(e0, ryb, FINE * nx, rzb, rcb, FINE * nx)
    send_x(("e", 0), e0)
    own_d0 = d0
    d0 = wide_fine(d0, ryb, 0, rzb, rcb, 0)
    send_x(("d", 0), d0)
    ec = e0
    local_e = local_operate(ec, ex, ey, ez, 2)
    local_d = local_operate(d0, cx, cy, cz, 1)
    ec = (ec + e0) - einv * operate(("e", 0), local_e, ec, be)
    send_x(("e", 1), ec)
    r1 = THETA * diag * d0 - operate(("d", 0), local_d, d0, bx)
    d1 = (RHO1 * RHO0) * d0 + (2.0 * RHO1 / DELTA) * r1 * inv
    send_x(("d", 1), d1)
    for j in range(1, sweeps):
        local_e = local_operate(ec, ex, ey, ez, 2)
        if j == sweeps - 1:
            local_d = local_operate(d1, cx, cy, cz, 1)
        ec = (ec + e0) - einv * operate(("e", j), local_e, ec, be)
        if j < sweeps - 1:
            send_x(("e", j + 1), ec)
    smooth = r1 - operate(("d", 1), local_d, d1, bx)
    smooth_ref[...] = smooth[:, :ny, :nz]
    base = u + own_d0 + d1[:, :ny, :nz]
    new = base.reshape(hx, 2, ny, nz) + ec[:, :ny, :nz][:, None]
    new_ref[...] = new.reshape(nx, ny, nz)

    for name, ways in exchanges.items():
        for d in ways:

            @pl.when(has(d))
            def _(name=name, d=d):
                copy(name, d).wait_send()


def on_device(sizes, right_side, conductivity, guess):
    nx, ny, nz = right_side.shape
    hx = nx // 2
    sweeps = KSWEEP - 1
    fine = (ny + 8, nz + LANES)
    coarse = (ny + 16, nz + LANES)
    rows_a = nx + FINE * nx + COARSE * hx
    rows_b = FINE * nx + COARSE * hx
    vmem = lambda *shape: pltpu.VMEM(shape, jnp.float32)
    block = jax.ShapeDtypeStruct((nx, ny, nz), jnp.float32)
    anywhere = pl.BlockSpec(memory_space=pl.ANY)
    inside = pl.BlockSpec(memory_space=pltpu.VMEM)
    messages = 2 + 8 + 8 + 2 + 4 + 2 * sweeps
    return pl.pallas_call(
        functools.partial(kernel, sizes),
        out_shape=(block, block),
        in_specs=[anywhere] * 3,
        out_specs=(inside, inside),
        scratch_shapes=[
            *[vmem(nx, ny, nz)] * 3,
            vmem(hx, ny, nz),
            vmem(nx, ny, nz),
            vmem(hx, ny, nz),
            *[vmem(2, 3, ny, nz)] * 2,
            *[vmem(2, rows_a, nz)] * 2,
            *[vmem(2, ny, LANES)] * 2,
            vmem(4, 8, LANES),
            *[vmem(2, rows_b, nz)] * 2,
            *[vmem(2, ny, LANES)] * 2,
            vmem(4, 8, LANES),
            *[vmem(2, fine[0] + coarse[0], fine[1])] * 2,
            *[vmem(2, 2, *fine)] * 2,
            *[vmem(sweeps, 2, *coarse)] * 2,
            pltpu.SemaphoreType.DMA((3,)),
            pltpu.SemaphoreType.DMA((messages,)),
            pltpu.SemaphoreType.DMA((messages,)),
        ],
        compiler_params=pltpu.CompilerParams(
            collective_id=0, has_side_effects=True, vmem_limit_bytes=60 * 1024 * 1024
        ),
        cost_estimate=pl.CostEstimate(
            flops=300 * nx * ny * nz, bytes_accessed=20 * nx * ny * nz, transcendentals=0
        ),
    )(right_side, conductivity, guess)


def solution(mesh):
    spec = P("pencil", "coarse", "gz")
    return jax.shard_map(
        functools.partial(on_device, tuple(mesh.shape[a] for a in AXES)),
        mesh=mesh,
        in_specs=(spec, spec, spec),
        out_specs=(spec, spec),
        check_vma=False,
    )
```

time: 22.7 us -> 21.2 us (0.934)
  local copies, waits for them, and re-layouts: 4.02 us -> 2.26 us
  Pallas kernels: 17.8 us -> 18.1 us
    unnamed x8 -> x4, local copies, waits for them, and re-layouts: 4.02 us -> 2.26 us
    pallas_call x1, Pallas kernels: 17.8 us -> 18.1 us  [on_device(): pl.pallas_call(functools.partial(kernel, sizes), out_shape=(block, block)...]
where the time goes in v2:
time: 21.2 us; the launch traced here: 21.1 us
  Pallas kernels  18.1 us (85%)
  local copies, waits for them, and re-layouts  2.26 us (11%)
  between operations  0.65 us (3%)
    pallas_call x1, Pallas kernels, on_device(): pl.pallas_call(functools.partial(kernel, sizes), out_shape=(block, block)...  18.1 us
    unnamed x4, local copies, waits for them, and re-layouts  2.26 us

profile of v2, /device:TPU:0, one launch (start us, length us, event | category | flops | bytes accessed | tf_op | source)
XLA Modules:
  0.0 21.1 jit_solution(11348009072800539844)
XLA Ops:
  0.6 18.1 %shard_map.50 = (f32[8,16,256]{2,1,0:T(8,128)}, f32[8,16,256]{2,1,0:T(8,128)}) custom-call(f32[8,16,256]{2,1,0:T(8,128)} %f_hbm.1, f32[8,16,256]{2,1,0:T(8,128)} %k_hbm.1, f32[8,16,256]{2,1,0:T(8,128)} %u_hbm.1), custom_call_target="tpu_custom_call" | custom-call | flops 9830400 | bytes 655360 | tf_op jit(solution)/shard_map/pallas_call | solution.py:422
  18.8 0.0 copy-start
  18.8 1.6 %copy.7 = f32[8,16,256]{2,1,0:T(8,128)} copy(f32[8,16,256]{2,1,0:T(8,128)} %get-tuple-element.4) | data formatting | bytes 262144
  20.4 0.0 copy-done
  20.4 0.7 %copy.8 = f32[8,16,256]{2,1,0:T(8,128)} copy(f32[8,16,256]{2,1,0:T(8,128)S(1)} %copy-done) | data formatting | bytes 262144
Async XLA Ops:
  18.8 1.6 %copy-start = (f32[8,16,256]{2,1,0:T(8,128)S(1)}, f32[8,16,256]{2,1,0:T(8,128)}, u32[]{:S(2)}) copy-start(f32[8,16,256]{2,1,0:T(8,128)} %get-tuple-element.5) | copy-start | bytes 393220

commit v3 on v2

--- a/solution.py
+++ b/solution.py
@@ -127,9 +127,9 @@
 
 
 def kernel(
-    sizes, f_hbm, k_hbm, u_hbm, new_ref, smooth_ref,
+    sizes, f_hbm, k_hbm, u_hbm, out_ref,
     f_ref, k_ref, u_ref, kc_ref, d_ref, e_ref,
-    sxa, rxa, sya, rya, sza, rza, rca,
+    sxa, rxa, sya, rya, syd, ryd, sza, rza, rca,
     syb, ryb, szb, rzb, rcb,
     sxk, rxk, sxd, rxd, sxe, rxe,
     in_sem, send_sem, recv_sem,
@@ -147,7 +147,7 @@
     def neighbour(d):
         return {AXES[i]: at[i] + c for i, c in enumerate(d) if c}
 
-    partners = X_WAYS + AROUND
+    partners = X_WAYS + Y_WAYS + Z_WAYS
     barrier = pltpu.get_barrier_semaphore()
     for d in partners:
 
@@ -165,9 +165,13 @@
     def x_ways(s, r):
         return {d: (s.at[i], r.at[i]) for i, d in enumerate(X_WAYS)}
 
-    def around(sy, ry, sz, rz, rc):
+    def faces(sy, ry, sz, rz):
         out = {d: (sy.at[i], ry.at[i]) for i, d in enumerate(Y_WAYS)}
         out.update({d: (sz.at[i], rz.at[i]) for i, d in enumerate(Z_WAYS)})
+        return out
+
+    def corners(sz, rc):
+        out = {}
         for i, d in enumerate(YZ_WAYS):
             rows = pl.ds(ny - 8 if d[1] > 0 else 0, 8)
             out[d] = (sz.at[1 if d[2] > 0 else 0, rows], rc.at[i])
@@ -175,8 +179,11 @@
 
     exchanges = {
         "first_x": x_ways(sxa, rxa),
-        "first": around(sya, rya, sza, rza, rca),
-        "second": around(syb, ryb, szb, rzb, rcb),
+        "first": faces(sya, rya, sza, rza),
+        "deep": {d: (syd.at[i], ryd.at[i]) for i, d in enumerate(Y_WAYS)},
+        "first_corner": corners(sza, rca),
+        "second_corner": corners(szb, rcb),
+        "second": faces(syb, ryb, szb, rzb),
         "k": x_ways(sxk, rxk),
     }
     for i in range(2):
@@ -188,7 +195,7 @@
         for d in ways:
             number[name, d] = len(number)
 
-    for way in partners:
+    for way in X_WAYS + AROUND:
 
         @pl.when(jnp.logical_not(has(way)))
         def _(way=way):
@@ -232,12 +239,13 @@
     row = lax.broadcasted_iota(jnp.int32, (1, ny, nz), 1)
     lane_even, row_even = lane % 2 == 0, row % 2 == 0
 
-    def put_rows(to, first, ref, depth, step, s):
+    def put_rows(to, first, ref, depths, step, s):
         n = ref.shape[0]
-        for r in range(depth):
+        for r in depths:
             y = ny - 1 - r * step if s else r * step
-            to[s, first + r * n : first + (r + 1) * n] = ref[:, y, :]
-        return first + depth * n
+            to[s, first : first + n] = ref[:, y, :]
+            first += n
+        return first
 
     loads[0].wait()
     k = k_ref[...]
@@ -250,13 +258,16 @@
         sxa[s, 0] = u[x]
         sxa[s, 1] = k[x]
         sxa[s, 2] = kc[x]
-        to = put_rows(sya, 0, u_ref, 1, 1, s)
-        to = put_rows(sya, to, k_ref, FINE, 1, s)
-        put_rows(sya, to, kc_ref, COARSE, 2, s)
+        to = put_rows(sya, 0, u_ref, (0,), 1, s)
+        to = put_rows(sya, to, k_ref, (0,), 1, s)
+        put_rows(sya, to, kc_ref, (0,), 2, s)
+        to = put_rows(syd, 0, k_ref, range(1, FINE), 1, s)
+        put_rows(syd, to, kc_ref, range(1, COARSE), 2, s)
         sza[s] = z_pack([(u, FINE), (k, FINE), (kc, 2 * COARSE)], s)
     pl.semaphore_wait(barrier, sum(has(d).astype(jnp.int32) for d in partners))
     send("first")
     send("first_x")
+    send("deep")
 
     def coefficients(k, step, scale, keep):
         cx = scale * (k[1:] + k[:-1])
@@ -292,6 +303,7 @@
 
     receive("first_x")
     receive("first")
+    send("first_corner")
 
     def first_halo(field, first_row, first_lane, width, n):
         return (
@@ -302,7 +314,7 @@
         )
 
     lane_k, lane_kc = FINE * nx, 2 * FINE * nx
-    row_k, row_kc = nx, nx + FINE * nx
+    row_k, row_kc = nx, 2 * nx
     ends = end_coefficients(k, first_halo(1, row_k, lane_k, FINE, nx), 1, 0.5)
     diag = with_ends(diag + ends[1] + ends[2], ends[0][0], ends[0][1])
     loads[2].wait()
@@ -314,15 +326,13 @@
     d_ref[...] = d0
     e_ref[...] = e0
     for s in range(2):
-        to = put_rows(syb, 0, d_ref, FINE, 1, s)
-        put_rows(syb, to, e_ref, COARSE, 2, s)
+        to = put_rows(syb, 0, d_ref, range(FINE), 1, s)
+        put_rows(syb, to, e_ref, range(COARSE), 2, s)
         szb[s] = z_pack([(d0, FINE), (e0, 2 * COARSE)], s)
+    send("second_corner")
     send("second")
 
-    def wide_fine(v, ry, first_row, rz, rc, first_lane):
-        def rows(i, r):
-            return ry[i, first_row + r * nx : first_row + (r + 1) * nx]
-
+    def wide_fine(v, rows, rz, rc, first_lane):
         near = [((r, r + 1), rows(1, r)) for r in range(FINE)]
         near += [((7 - r, 8 - r), rows(0, r)) for r in range(FINE)]
         tall = jnp.concatenate([v, tile_of(near, (nx, nz))], 1)
@@ -333,18 +343,23 @@
             ends.append(jnp.concatenate([rz[i], corner], 0))
         return jnp.concatenate([tall, z_unpack(ends[0], ends[1], first_lane, FINE, nx)], 2)
 
-    def wide_coarse(v, ry, first_row, rz, rc, first_lane):
-        def rows(i, r):
-            return ry[i, first_row + r * hx : first_row + (r + 1) * hx]
-
+    def wide_coarse(v, rows, rz, rc, first_lane):
         high = tile_of([((2 * r, 2 * r + 2), rows(1, r)) for r in range(COARSE)], (hx, nz))
         low = tile_of([((6 - 2 * r, 8 - 2 * r), rows(0, r)) for r in range(COARSE)], (hx, nz))
         tall = jnp.concatenate([v, high, low], 1)
         ends = [jnp.concatenate([rz[i], rc[2 + i], rc[i]], 0) for i in range(2)]
         return jnp.concatenate([tall, z_unpack(ends[0], ends[1], first_lane, 2 * COARSE, hx)], 2)
 
-    wk = wide_fine(k, rya, row_k, rza, rca, lane_k)
-    wkc = wide_coarse(kc, rya, row_kc, rza, rca, lane_kc)
+    def rows_of(ref, first, n):
+        return lambda i, r: ref[i, first + r * n : first + (r + 1) * n]
+
+    def first_or_deep(first, deep, n):
+        return lambda i, r: (rows_of(ryd, deep, n)(i, r - 1) if r else rows_of(rya, first, n)(i, 0))
+
+    receive("deep")
+    receive("first_corner")
+    wk = wide_fine(k, first_or_deep(row_k, 0, nx), rza, rca, lane_k)
+    wkc = wide_coarse(kc, first_or_deep(row_kc, (FINE - 1) * nx, hx), rza, rca, lane_kc)
     fine_rows = wk.shape[1]
     for s in range(2):
         x = -1 if s else 0
@@ -372,10 +387,11 @@
         return with_ends(local, b[0] * (v[:1] - low), b[1] * (v[-1:] - high))
 
     receive("second")
-    e0 = wide_coarse(e0, ryb, FINE * nx, rzb, rcb, FINE * nx)
+    receive("second_corner")
+    e0 = wide_coarse(e0, rows_of(ryb, FINE * nx, hx), rzb, rcb, FINE * nx)
     send_x(("e", 0), e0)
     own_d0 = d0
-    d0 = wide_fine(d0, ryb, 0, rzb, rcb, 0)
+    d0 = wide_fine(d0, rows_of(ryb, 0, nx), rzb, rcb, 0)
     send_x(("d", 0), d0)
     ec = e0
     local_e = local_operate(ec, ex, ey, ez, 2)
@@ -393,10 +409,10 @@
         if j < sweeps - 1:
             send_x(("e", j + 1), ec)
     smooth = r1 - operate(("d", 1), local_d, d1, bx)
-    smooth_ref[...] = smooth[:, :ny, :nz]
+    out_ref[1] = smooth[:, :ny, :nz]
     base = u + own_d0 + d1[:, :ny, :nz]
     new = base.reshape(hx, 2, ny, nz) + ec[:, :ny, :nz][:, None]
-    new_ref[...] = new.reshape(nx, ny, nz)
+    out_ref[0] = new.reshape(nx, ny, nz)
 
     for name, ways in exchanges.items():
         for d in ways:
@@ -412,18 +428,19 @@
     sweeps = KSWEEP - 1
     fine = (ny + 8, nz + LANES)
     coarse = (ny + 16, nz + LANES)
-    rows_a = nx + FINE * nx + COARSE * hx
+    rows_a = 2 * nx + hx
+    rows_d = (FINE - 1) * nx + (COARSE - 1) * hx
     rows_b = FINE * nx + COARSE * hx
     vmem = lambda *shape: pltpu.VMEM(shape, jnp.float32)
     block = jax.ShapeDtypeStruct((nx, ny, nz), jnp.float32)
     anywhere = pl.BlockSpec(memory_space=pl.ANY)
     inside = pl.BlockSpec(memory_space=pltpu.VMEM)
-    messages = 2 + 8 + 8 + 2 + 4 + 2 * sweeps
-    return pl.pallas_call(
+    messages = 2 + 4 + 2 + 4 + 4 + 4 + 2 + 4 + 2 * sweeps
+    both = pl.pallas_call(
         functools.partial(kernel, sizes),
-        out_shape=(block, block),
+        out_shape=jax.ShapeDtypeStruct((2, nx, ny, nz), jnp.float32),
         in_specs=[anywhere] * 3,
-        out_specs=(inside, inside),
+        out_specs=inside,
         scratch_shapes=[
             *[vmem(nx, ny, nz)] * 3,
             vmem(hx, ny, nz),
@@ -431,6 +448,7 @@
             vmem(hx, ny, nz),
             *[vmem(2, 3, ny, nz)] * 2,
             *[vmem(2, rows_a, nz)] * 2,
+            *[vmem(2, rows_d, nz)] * 2,
             *[vmem(2, ny, LANES)] * 2,
             vmem(4, 8, LANES),
             *[vmem(2, rows_b, nz)] * 2,
@@ -450,6 +468,7 @@
             flops=300 * nx * ny * nz, bytes_accessed=20 * nx * ny * nz, transcendentals=0
         ),
     )(right_side, conductivity, guess)
+    return both[0], both[1]
 
 
 def solution(mesh):

time: 21.2 us -> 19.5 us (0.920)
  Pallas kernels: 18.1 us -> 17 us
  local copies, waits for them, and re-layouts: 2.26 us -> 1.69 us
    unnamed x4 -> x0, local copies, waits for them, and re-layouts: 2.26 us -> none
    squeeze x0 -> x1, local copies, waits for them, and re-layouts: none -> 1.69 us  [on_device(): return (both[0], both[1])]
    pallas_call x1, Pallas kernels: 18.1 us -> 17 us  [on_device(): pl.pallas_call(functools.partial(kernel, sizes), out_shape=jax.ShapeDtype...]
where the time goes in v3:
time: 19.5 us; the launch traced here: 19.4 us
  Pallas kernels  17 us (87%)
  local copies, waits for them, and re-layouts  1.69 us (9%)
  between operations  0.64 us (3%)
    pallas_call x1, Pallas kernels, on_device(): pl.pallas_call(functools.partial(kernel, sizes), out_shape=jax.ShapeDtype...  17 us
    squeeze x1, local copies, waits for them, and re-layouts, on_device(): return (both[0], both[1])  1.69 us

profile of v3, /device:TPU:0, one launch (start us, length us, event | category | flops | bytes accessed | tf_op | source)
XLA Modules:
  0.0 19.4 jit_solution(15431426783328321104)
XLA Ops:
  0.6 17.0 %shard_map.50 = f32[2,8,16,256]{3,2,1,0:T(8,128)} custom-call(f32[8,16,256]{2,1,0:T(8,128)} %f_hbm.1, f32[8,16,256]{2,1,0:T(8,128)} %k_hbm.1, f32[8,16,256]{2,1,0:T(8,128)} %u_hbm.1), custom_call_target="tpu_custom_call" | custom-call | flops 9830400 | bytes 655360 | tf_op jit(solution)/shard_map/pallas_call | solution.py:439
  17.7 1.7 %slice_bitcast_fusion = (f32[8,16,256]{2,1,0:T(8,128)}, f32[8,16,256]{2,1,0:T(8,128)}) fusion(f32[2,8,16,256]{3,2,1,0:T(8,128)} %shard_map.50), kind=kLoop, calls=%fused_computation | loop fusion | bytes 524288 | tf_op jit(solution)/shard_map/squeeze | solution.py:471
